TPU v7x, 32 devices: a whole 2x2x4 slice. The times are simulated.
32 devices in a mesh: rep: 4 (over z), node: 4 (over y, core), local: 2 (over x).
Axes of the slice: x: 2, y: 2, z: 4, core: 2. Of those that a mesh axis runs over, the one named last changes fastest.
Arguments:
- tokens: bfloat16 [2048, 7168], P(('rep', 'node', 'local')), parts along dimension 0, may hold values from -6 to 6
- expert_ids: int32 [2048, 8], P(('rep', 'node', 'local')), parts along dimension 0, may hold values from 0 to 31, as said below
- node_groups: int32 [2048, 2], P(('rep', 'node', 'local')), parts along dimension 0, may hold values from 0 to 3, as said below
- gate_levels: int32 [2048, 8], P(('rep', 'node', 'local')), parts along dimension 0, may hold values from 1 to 255
- expert_seeds: int32 [32], P(('node', 'local')), may hold values from 0 to 999999999
Outputs:
- routed_out: bfloat16 [2048, 7168], P(('rep', 'node', 'local')), parts along dimension 0
There are 4 independent parts, one for each index of `rep`. A program takes and returns all parts, laid end to end along the dimension named above; an argument that names none is the same for every part. Nothing has to cross between parts.
Inputs may be any that keep to these rules, and one draw needn't show every extreme that they name: `expert_ids`: each row names 8 different experts; expert e belongs to node group e // 8. `node_groups`: each row names 2 different node groups.
All inputs are finite; a program needn't handle non-finite values.
Results may differ from a plain program's by a relative error of at most 0.0085.
Values may be sent and summed in bfloat16 or wider, within the bound.
A program may use at most 192 MiB of HBM per device.

v0:
```python
import math

import jax
import jax.numpy as jnp
from jax import lax
from jax.sharding import PartitionSpec as P

D = 7168
FF = 1024
TOP = 8
EXP_DEV = 4


route_scale = 2.5
salt_gate = 1013904223
salt_up = 1664525
salt_down = 22695477


def hashed_weight(expert_seed, salt_value, row_count, column_count, fan_in):
    row_index = lax.broadcasted_iota(jnp.int32, (row_count, column_count), 0)
    column_index = lax.broadcasted_iota(jnp.int32, (row_count, column_count), 1)
    hashed = (
        (row_index * column_count + column_index) * 747796405
        + expert_seed * 1103515245
        + salt_value
    )
    hashed = hashed ^ hashed >> 15
    hashed = hashed * 277803737
    hashed = hashed ^ hashed >> 13
    hashed = hashed * 668265263
    hashed = hashed ^ hashed >> 16
    sixteen_bits = (hashed >> 8 & 65535).astype(jnp.float32)
    return ((sixteen_bits - 32767.5) * (math.sqrt(3.0 / fan_in) / 32768.0)).astype(jnp.bfloat16)


def expert_block(block_rows, expert_seed):
    weight_gate = hashed_weight(expert_seed, salt_gate, D, FF, D)
    weight_up = hashed_weight(expert_seed, salt_up, D, FF, D)
    weight_down = hashed_weight(expert_seed, salt_down, FF, D, FF)
    gate_part = jnp.dot(block_rows, weight_gate, preferred_element_type=jnp.float32)
    up_part = jnp.dot(block_rows, weight_up, preferred_element_type=jnp.float32)
    hidden = (jax.nn.silu(gate_part) * up_part).astype(jnp.bfloat16)
    return jnp.dot(hidden, weight_down, preferred_element_type=jnp.float32).astype(jnp.bfloat16)


def run_experts(expert_rows, local_seeds):

    def per_expert(running, scan_item):
        expert_seed, block_rows = scan_item
        return (running, expert_block(block_rows, expert_seed))

    unused, outputs = lax.scan(per_expert, jnp.zeros((), jnp.int32), (local_seeds, expert_rows))
    return outputs


def group_mask(expert_ids, node_groups, group_size):
    return jnp.any((expert_ids // group_size)[:, :, None] == node_groups[:, None, :], axis=2)


def gate_of(gate_levels, in_group):
    levels = gate_levels.astype(jnp.float32)
    return (
        route_scale * levels * in_group.astype(jnp.float32) / jnp.sum(levels, axis=1, keepdims=True)
    )


def rank_of(expert_ids, in_group, blocks, capacity, experts_total):
    expert_range = jnp.arange(experts_total, dtype=jnp.int32)
    hit_table = (
        (expert_ids[:, :, None] == expert_range[None, None, :]) & in_group[:, :, None]
    ).astype(jnp.int32)
    present = jnp.sum(hit_table, axis=1, dtype=jnp.int32)
    blocked = present.reshape(blocks, -1, experts_total)
    before = (jnp.cumsum(blocked, axis=1, dtype=jnp.int32) - blocked).reshape(-1, experts_total)
    slot_rank = jnp.sum(hit_table * before[:, None, :], axis=2, dtype=jnp.int32)
    kept_mask = in_group & (slot_rank < capacity)
    return (slot_rank, kept_mask)


def fill_slots(row_block, slot_index, slot_total):
    row_count = row_block.shape[0]
    token_index = lax.broadcasted_iota(jnp.int32, slot_index.shape, 0)
    slot_token = (
        jnp.full((slot_total,), row_count, jnp.int32)
        .at[slot_index.reshape(-1)]
        .set(token_index.reshape(-1), mode="drop")
    )
    padded = jnp.concatenate(
        [row_block, jnp.zeros((1, row_block.shape[1]), row_block.dtype)], axis=0
    )
    return padded[slot_token]


def combine_rows(returned, slot_index, gate_share):
    padded = jnp.concatenate([returned, jnp.zeros((1, returned.shape[1]), returned.dtype)], axis=0)
    picked = padded[slot_index]
    return jnp.einsum("tj,tjd->td", gate_share, picked.astype(jnp.float32))


def on_device(tokens, expert_ids, node_groups, gate_levels, expert_seeds):
    tok_count = tokens.shape[0]
    width = tokens.shape[1]
    devices_all = lax.axis_size(("node", "local"))
    local_count = lax.axis_size("local")
    experts_total = EXP_DEV * devices_all
    capacity = max(2, tok_count * TOP // experts_total)
    group_size = EXP_DEV * local_count
    in_group = group_mask(expert_ids, node_groups, group_size)
    gate_share = gate_of(gate_levels, in_group)
    slot_rank, kept_mask = rank_of(expert_ids, in_group, 1, capacity, experts_total)
    slot_total = experts_total * capacity
    slot_index = jnp.where(kept_mask, expert_ids * capacity + slot_rank, slot_total)
    send_rows = fill_slots(tokens, slot_index, slot_total).reshape(
        devices_all, EXP_DEV, capacity, width
    )
    arrived = lax.all_to_all(send_rows, ("node", "local"), split_axis=0, concat_axis=2, tiled=True)
    results = run_experts(arrived.reshape(EXP_DEV, -1, width), expert_seeds)
    returned = lax.all_to_all(
        results.reshape(1, EXP_DEV, -1, width),
        ("node", "local"),
        split_axis=2,
        concat_axis=0,
        tiled=True,
    )
    return combine_rows(returned.reshape(slot_total, width), slot_index, gate_share).astype(
        jnp.bfloat16
    )


def solution(mesh):
    in_specs = (
        P(("rep", "node", "local"), None),
        P(("rep", "node", "local"), None),
        P(("rep", "node", "local"), None),
        P(("rep", "node", "local"), None),
        P(("node", "local")),
    )
    out_specs = P(("rep", "node", "local"), None)
    return jax.shard_map(
        on_device, mesh=mesh, in_specs=in_specs, out_specs=out_specs, check_vma=False
    )
```

profile of v0, /device:TPU:0, one launch (start us, length us, event | category | flops | bytes accessed | tf_op | source)
XLA Modules:
  0.0 496.6 jit_solution(14484144332202261797)
XLA Ops:
  0.0 0.7 add_select_fusion
  0.7 0.7 compare_reduce_fusion
  1.4 0.0 copy-start
  1.4 0.7 convert_reduce_fusion
  2.1 0.1 copy.29
  2.2 0.1 reduce_window_sum.11
  2.3 0.1 copy.31
  2.4 0.7 select_reduce_fusion
  3.1 1.3 compare_select_fusion.1
  4.4 0.1 copy.32
  4.5 0.1 reshape.69
  4.6 0.1 reshape.95
  4.7 2.4 scatter_custom_fusion
  7.1 0.0 copy-done
  7.2 1.2 concatenate.6
  8.4 7.1 %gather_fusion = bf16[512,7168]{1,0:T(8,128)(2,1)} fusion(bf16[65,7168]{1,0:T(8,128)(2,1)S(1)} %concatenate.6, s32[1024]{0:T(1024)S(1)} %pad_clamp_fusion.1), kind=kCustom, calls=%fused_computation | custom fusion | bytes 14682112 | tf_op jit(solution)/shard_map/gather | solution.py:92
  15.5 5.2 %all-to-all-start = ((bf16[8,4,16,7168]{3,2,1,0:T(8,128)(2,1)}), bf16[8,4,16,7168]{3,2,1,0:T(8,128)(2,1)}, u32[]{:S(2)}, u32[]{:S(2)}) async-start(bf16[8,4,16,7168]{3,2,1,0:T(8,128)(2,1)} %bitcast.47), calls=%async_computation | async-start | bytes 14680064 | tf_op jit(solution)/shard_map/all_to_all | solution.py:117
  20.6 0.0 copy-start.4
  20.6 82.3 %all-to-all-done = bf16[8,4,16,7168]{3,2,1,0:T(8,128)(2,1)} async-done(((bf16[8,4,16,7168]{3,2,1,0:T(8,128)(2,1)}), bf16[8,4,16,7168]{3,2,1,0:T(8,128)(2,1)}, u32[]{:S(2)}, u32[]{:S(2)}) %all-to-all-start) | async-done | bytes 7340064 | tf_op jit(solution)/shard_map/all_to_all | solution.py:117
  103.0 6.8 %copy.33 = bf16[1,4,8,16,7168]{4,3,2,1,0:T(8,128)(2,1)} copy(bf16[1,4,8,16,7168]{4,3,1,2,0:T(8,128)(2,1)} %bitcast.7) | data formatting | bytes 14680064 | tf_op jit(solution)/shard_map/all_to_all | solution.py:117
  109.8 0.0 copy-done.4
  109.8 253.5 %while.13 = (s32[]{:T(128)}, bf16[4,128,7168]{2,1,0:T(8,128)(2,1)}, bf16[4,128,7168]{2,1,0:T(8,128)(2,1)}, s32[4]{0:T(128)S(1)}, s32[]{:T(128)}, /*index=5*/s32[1]{0:T(128)}) while((s32[]{:T(128)}, bf16[4,128,7168]{2,1,0:T(8,128)(2,1)}, bf16[4,128,7168]{2,1,0:T(8,128)(2,1)}, s32[4]{0:T(128)S(1)}, s32[]{:T(128)}, /*index=5*/s32[1]{0:T(128)}) %tuple.34), condition=%wide.region_7.8_spmd, body=%wide.region_6.7_spmd.sunk | while | flops 6035218432 | bytes 7175261 | solution.py:53
  110.3 0.7 dynamic_slice.33
  111.6 19.9 %fusion.112 = f32[128,1024]{1,0:T(8,128)S(1)} fusion(s32[]{:T(128)} %bitcast.46, s32[7168]{0:T(1024)S(1)} %iota_multiply_fusion.4, bf16[4,128,7168]{2,1,0:T(8,128)(2,1)} %get-tuple-element.123, s32[]{:T(128)} %get-tuple-element.115), kind=kOutput, calls=%fused_computation.39.clone.1 | convolution fusion | flops 2011168768 | bytes 2388992 | tf_op jit(solution)/shard_map/while/body/eval_jaxpr/dot_general | solution.py:41
  131.5 20.4 %fusion.113 = bf16[128,1024]{1,0:T(8,128)(2,1)S(1)} fusion(s32[]{:T(128)} %bitcast.46, s32[7168]{0:T(1024)S(1)} %iota_multiply_fusion.4, bf16[4,128,7168]{2,1,0:T(8,128)(2,1)} %get-tuple-element.123, s32[]{:T(128)} %get-tuple-element.115, f32[128,1024]{1,0:T(8,128)S(1)} %fusion.112), kind=kOutput, calls=%fused_computation.48.clone.1 | convolution fusion | flops 2011955200 | bytes 2651136 | tf_op jit(solution)/shard_map/while/body/eval_jaxpr/dot_general | solution.py:42
  151.9 20.3 %fusion.114 = bf16[4,128,7168]{2,1,0:T(8,128)(2,1)} fusion(bf16[4,128,7168]{2,1,0:T(8,128)(2,1)} %get-tuple-element.116, s32[]{:T(128)} %get-tuple-element.115, bf16[128,1024]{1,0:T(8,128)(2,1)S(1)} %fusion.113, s32[]{:T(128)} %bitcast.46, s32[1024]{0:T(1024)S(1)} %iota_multiply_fusion.5), kind=kOutput, calls=%fused_computation.42.clone.1 | convolution fusion | flops 2012086272 | bytes 2102272 | tf_op jit(solution)/shard_map/while/body/eval_jaxpr/dot_general | solution.py:44
  172.3 0.7 dynamic_slice.33
  173.6 20.1 %fusion.112 = f32[128,1024]{1,0:T(8,128)S(1)} fusion(s32[]{:T(128)} %bitcast.46, s32[7168]{0:T(1024)S(1)} %iota_multiply_fusion.4, bf16[4,128,7168]{2,1,0:T(8,128)(2,1)} %get-tuple-element.123, s32[]{:T(128)} %get-tuple-element.115), kind=kOutput, calls=%fused_computation.39.clone.1 | convolution fusion | flops 2011168768 | bytes 2388992 | tf_op jit(solution)/shard_map/while/body/eval_jaxpr/dot_general | solution.py:41
  193.7 20.1 %fusion.113 = bf16[128,1024]{1,0:T(8,128)(2,1)S(1)} fusion(s32[]{:T(128)} %bitcast.46, s32[7168]{0:T(1024)S(1)} %iota_multiply_fusion.4, bf16[4,128,7168]{2,1,0:T(8,128)(2,1)} %get-tuple-element.123, s32[]{:T(128)} %get-tuple-element.115, f32[128,1024]{1,0:T(8,128)S(1)} %fusion.112), kind=kOutput, calls=%fused_computation.48.clone.1 | convolution fusion | flops 2011955200 | bytes 2651136 | tf_op jit(solution)/shard_map/while/body/eval_jaxpr/dot_general | solution.py:42
  213.9 20.4 %fusion.114 = bf16[4,128,7168]{2,1,0:T(8,128)(2,1)} fusion(bf16[4,128,7168]{2,1,0:T(8,128)(2,1)} %get-tuple-element.116, s32[]{:T(128)} %get-tuple-element.115, bf16[128,1024]{1,0:T(8,128)(2,1)S(1)} %fusion.113, s32[]{:T(128)} %bitcast.46, s32[1024]{0:T(1024)S(1)} %iota_multiply_fusion.5), kind=kOutput, calls=%fused_computation.42.clone.1 | convolution fusion | flops 2012086272 | bytes 2102272 | tf_op jit(solution)/shard_map/while/body/eval_jaxpr/dot_general | solution.py:44
  234.5 0.7 dynamic_slice.33
  235.8 19.9 %fusion.112 = f32[128,1024]{1,0:T(8,128)S(1)} fusion(s32[]{:T(128)} %bitcast.46, s32[7168]{0:T(1024)S(1)} %iota_multiply_fusion.4, bf16[4,128,7168]{2,1,0:T(8,128)(2,1)} %get-tuple-element.123, s32[]{:T(128)} %get-tuple-element.115), kind=kOutput, calls=%fused_computation.39.clone.1 | convolution fusion | flops 2011168768 | bytes 2388992 | tf_op jit(solution)/shard_map/while/body/eval_jaxpr/dot_general | solution.py:41
  255.7 20.3 %fusion.113 = bf16[128,1024]{1,0:T(8,128)(2,1)S(1)} fusion(s32[]{:T(128)} %bitcast.46, s32[7168]{0:T(1024)S(1)} %iota_multiply_fusion.4, bf16[4,128,7168]{2,1,0:T(8,128)(2,1)} %get-tuple-element.123, s32[]{:T(128)} %get-tuple-element.115, f32[128,1024]{1,0:T(8,128)S(1)} %fusion.112), kind=kOutput, calls=%fused_computation.48.clone.1 | convolution fusion | flops 2011955200 | bytes 2651136 | tf_op jit(solution)/shard_map/while/body/eval_jaxpr/dot_general | solution.py:42
  276.0 20.2 %fusion.114 = bf16[4,128,7168]{2,1,0:T(8,128)(2,1)} fusion(bf16[4,128,7168]{2,1,0:T(8,128)(2,1)} %get-tuple-element.116, s32[]{:T(128)} %get-tuple-element.115, bf16[128,1024]{1,0:T(8,128)(2,1)S(1)} %fusion.113, s32[]{:T(128)} %bitcast.46, s32[1024]{0:T(1024)S(1)} %iota_multiply_fusion.5), kind=kOutput, calls=%fused_computation.42.clone.1 | convolution fusion | flops 2012086272 | bytes 2102272 | tf_op jit(solution)/shard_map/while/body/eval_jaxpr/dot_general | solution.py:44
  296.6 0.7 dynamic_slice.33
  297.9 19.9 %fusion.112 = f32[128,1024]{1,0:T(8,128)S(1)} fusion(s32[]{:T(128)} %bitcast.46, s32[7168]{0:T(1024)S(1)} %iota_multiply_fusion.4, bf16[4,128,7168]{2,1,0:T(8,128)(2,1)} %get-tuple-element.123, s32[]{:T(128)} %get-tuple-element.115), kind=kOutput, calls=%fused_computation.39.clone.1 | convolution fusion | flops 2011168768 | bytes 2388992 | tf_op jit(solution)/shard_map/while/body/eval_jaxpr/dot_general | solution.py:41
  317.8 20.4 %fusion.113 = bf16[128,1024]{1,0:T(8,128)(2,1)S(1)} fusion(s32[]{:T(128)} %bitcast.46, s32[7168]{0:T(1024)S(1)} %iota_multiply_fusion.4, bf16[4,128,7168]{2,1,0:T(8,128)(2,1)} %get-tuple-element.123, s32[]{:T(128)} %get-tuple-element.115, f32[128,1024]{1,0:T(8,128)S(1)} %fusion.112), kind=kOutput, calls=%fused_computation.48.clone.1 | convolution fusion | flops 2011955200 | bytes 2651136 | tf_op jit(solution)/shard_map/while/body/eval_jaxpr/dot_general | solution.py:42
  338.2 20.2 %fusion.114 = bf16[4,128,7168]{2,1,0:T(8,128)(2,1)} fusion(bf16[4,128,7168]{2,1,0:T(8,128)(2,1)} %get-tuple-element.116, s32[]{:T(128)} %get-tuple-element.115, bf16[128,1024]{1,0:T(8,128)(2,1)S(1)} %fusion.113, s32[]{:T(128)} %bitcast.46, s32[1024]{0:T(1024)S(1)} %iota_multiply_fusion.5), kind=kOutput, calls=%fused_computation.42.clone.1 | convolution fusion | flops 2012086272 | bytes 2102272 | tf_op jit(solution)/shard_map/while/body/eval_jaxpr/dot_general | solution.py:44
  363.3 11.7 %copy.41 = bf16[4,128,7168]{2,0,1:T(4,128)(2,1)} copy(bf16[4,128,7168]{2,1,0:T(8,128)(2,1)} %get-tuple-element.73) | data formatting | bytes 14680064 | tf_op jit(solution)/shard_map/while | solution.py:53
  375.0 0.0 copy-start.2
  375.0 0.0 copy-start.3
  375.0 0.0 copy-start.1
  375.0 5.4 %all-to-all-start.1 = ((bf16[1,4,128,7168]{3,1,0,2:T(4,128)(2,1)}), bf16[1,4,128,7168]{3,1,0,2:T(4,128)(2,1)}, u32[]{:S(2)}, u32[]{:S(2)}) async-start(bf16[1,4,128,7168]{3,1,0,2:T(4,128)(2,1)} %bitcast.49), calls=%async_computation.1 | async-start | bytes 14680064 | tf_op jit(solution)/shard_map/all_to_all | solution.py:119
  380.5 0.0 copy-done.2
  380.5 0.1 copy.36
  380.6 0.1 reshape.85
  380.7 0.0 copy-done.3
  380.7 0.0 copy-done.1
  380.7 0.1 copy.37
  380.8 82.0 %all-to-all-done.1 = bf16[1,4,128,7168]{3,1,0,2:T(4,128)(2,1)} async-done(((bf16[1,4,128,7168]{3,1,0,2:T(4,128)(2,1)}), bf16[1,4,128,7168]{3,1,0,2:T(4,128)(2,1)}, u32[]{:S(2)}, u32[]{:S(2)}) %all-to-all-start.1) | async-done | bytes 7340064 | tf_op jit(solution)/shard_map/all_to_all | solution.py:119
  462.8 5.4 %copy.35 = bf16[1,4,8,16,7168]{4,3,1,2,0:T(8,128)(2,1)S(1)} copy(bf16[1,4,8,16,7168]{4,1,3,2,0:T(4,128)(2,1)} %bitcast.10) | data formatting | bytes 14680064 | tf_op jit(solution)/shard_map/all_to_all | solution.py:119
  468.2 3.8 concatenate.7
  472.0 18.1 %gather_fusion.1 = bf16[512,7168]{1,0:T(8,128)(2,1)} fusion(bf16[513,7168]{1,0:T(8,128)(2,1)} %concatenate.7, s32[1024]{0:T(1024)S(1)} %pad_clamp_fusion), kind=kCustom, calls=%fused_computation.1 | custom fusion | bytes 14682112 | tf_op jit(solution)/shard_map/gather | solution.py:97
  490.1 5.1 %fusion.88 = bf16[64,1,7168]{2,1,0:T(2,128)(2,1)S(1)} fusion(bf16[64,8,1]{1,2,0:T(2,128)(2,1)S(1)} %copy.37, bf16[512,7168]{1,0:T(8,128)(2,1)} %gather_fusion.1), kind=kOutput, calls=%fused_computation.86 | convolution fusion | flops 7340032 | bytes 8258560 | tf_op jit(solution)/shard_map/tj,tjd->td/dot_general | solution.py:98
  495.2 1.2 copy.42
  (17 shorter events, 0.1 us)
Async XLA Ops:
  1.4 5.8 %copy-start = (pred[64,8]{0,1:T(8,128)(4,1)}, pred[64,8]{0,1:T(8,128)(4,1)S(1)}, u32[]{:S(2)}) copy-start(pred[64,8]{0,1:T(8,128)(4,1)S(1)} %compare_reduce_fusion) | copy-start | bytes 1540
  15.5 87.5 %all-to-all-start = ((bf16[8,4,16,7168]{3,2,1,0:T(8,128)(2,1)}), bf16[8,4,16,7168]{3,2,1,0:T(8,128)(2,1)}, u32[]{:S(2)}, u32[]{:S(2)}) async-start(bf16[8,4,16,7168]{3,2,1,0:T(8,128)(2,1)} %bitcast.47), calls=%async_computation | async-start | bytes 14680064 | tf_op jit(solution)/shard_map/all_to_all | solution.py:117
  20.6 89.1 %copy-start.4 = (s32[4]{0:T(128)S(1)}, s32[4]{0:T(128)}, u32[]{:S(2)}) copy-start(s32[4]{0:T(128)} %param.11) | copy-start | bytes 52
  375.0 5.4 %copy-start.2 = (s32[64,8]{0,1:T(8,128)S(1)}, s32[64,8]{0,1:T(8,128)}, u32[]{:S(2)}) copy-start(s32[64,8]{0,1:T(8,128)} %get-tuple-element.82) | copy-start | bytes 6148
  375.0 5.6 %copy-start.3 = (s32[64,8]{0,1:T(8,128)S(1)}, s32[64,8]{0,1:T(8,128)}, u32[]{:S(2)}) copy-start(s32[64,8]{0,1:T(8,128)} %param.10) | copy-start | bytes 6148
  375.0 5.7 %copy-start.1 = (pred[64,8]{0,1:T(8,128)(4,1)S(1)}, pred[64,8]{0,1:T(8,128)(4,1)}, u32[]{:S(2)}) copy-start(pred[64,8]{0,1:T(8,128)(4,1)} %copy-done) | copy-start | bytes 1540
  375.0 87.8 %all-to-all-start.1 = ((bf16[1,4,128,7168]{3,1,0,2:T(4,128)(2,1)}), bf16[1,4,128,7168]{3,1,0,2:T(4,128)(2,1)}, u32[]{:S(2)}, u32[]{:S(2)}) async-start(bf16[1,4,128,7168]{3,1,0,2:T(4,128)(2,1)} %bitcast.49), calls=%async_computation.1 | async-start | bytes 14680064 | tf_op jit(solution)/shard_map/all_to_all | solution.py:119
where the time goes:
time: 501 us; the launch traced here: 497 us
  matrix products  247 us (49%)
  waiting for transfers between devices  164 us (33%)
  local copies, waits for them, and re-layouts  61.1 us (12%)
  starting transfers between devices  10.6 us (2%)
  loops' own time  8.94 us (2%)
    all_to_all x1, waiting for transfers between devices, on_device(): lax.all_to_all(send_rows, ('node', 'local'), split_axis=0, concat_axis=2,...  82.3 us
    all_to_all x1, waiting for transfers between devices, on_device(): lax.all_to_all(results.reshape(1, EXP_DEV, -1, width), ('node', 'local'),...  82 us
    dot_general x4, matrix products, expert_block(): up_part = jnp.dot(block_rows, weight_up, preferred_element_type=jnp.float32)  81.2 us
    dot_general x4, matrix products, expert_block(): jnp.dot(hidden, weight_down, preferred_element_type=jnp.float32)  81.1 us
    dot_general x4, matrix products, expert_block(): jnp.dot(block_rows, weight_gate, preferred_element_type=jnp.float32)  79.7 us
    gather x1, local copies, waits for them, and re-layouts, combine_rows(): picked = padded[slot_index]  18.1 us
    while x1, local copies, waits for them, and re-layouts, run_experts(): lax.scan(per_expert, jnp.zeros((), jnp.int32), (local_seeds, expert_rows))  11.7 us
  transfers between devices with their start and end apart: 2, of which 2 were waited for; matrix products, arithmetic and copies ran while one was open for 0% of the time, Pallas kernels for 0%

commit v1 on v0

v1 whole, which is shorter than its diff:
```python
import functools
import math

import jax
import jax.numpy as jnp
from jax import lax
from jax.experimental import pallas as pl
from jax.experimental.pallas import tpu as pltpu
from jax.sharding import PartitionSpec as P

D = 7168
FF = 1024
TOP = 8
EXP_DEV = 4
AXES = ("node", "local")

route_scale = 2.5
salt_gate = 1013904223
salt_up = 1664525
salt_down = 22695477
INDEX_MUL = 747796405
SEED_MUL = 1103515245
SCALE_IN = math.sqrt(3.0 / D) / 32768.0
SCALE_OUT = math.sqrt(3.0 / FF) / 32768.0

ROWS = 512
COLS = 256
DOWN_COLS = 256
CHUNKS = 4


def as_int32(value):
    return jnp.int32((value + 2**31) % 2**32 - 2**31)


def centred(hashed):
    hashed = hashed ^ (hashed >> 15)
    hashed = hashed * jnp.int32(277803737)
    hashed = hashed ^ (hashed >> 13)
    hashed = hashed * jnp.int32(668265263)
    hashed = hashed ^ (hashed >> 16)
    sixteen = (hashed >> 8) & jnp.int32(65535)
    return (sixteen.astype(jnp.float32) - 32767.5).astype(jnp.bfloat16)


def fill_index(lin, columns):
    row = lax.broadcasted_iota(jnp.int32, lin.shape, 0)
    col = lax.broadcasted_iota(jnp.int32, lin.shape, 1)
    lin[...] = (row * columns + col) * as_int32(INDEX_MUL)


def offset(seed, salt, row, col, columns):
    return (row * columns + col) * as_int32(INDEX_MUL) + seed * as_int32(SEED_MUL) + jnp.int32(salt)


def make_kernel(seeds, gate_out, up_out, lin):
    tile = pl.program_id(0)

    @pl.when(tile == 0)
    def _():
        fill_index(lin, FF)

    @pl.loop(0, D // ROWS)
    def _(step):
        rows = pl.ds(pl.multiple_of(step * ROWS, ROWS), ROWS)
        for salt, out in ((salt_gate, gate_out), (salt_up, up_out)):
            out[rows, :] = centred(lin[...] + offset(seeds[0], salt, step * ROWS, tile * COLS, FF))


def make_weights(seeds):
    spec = pl.BlockSpec((D, COLS), lambda t: (0, t))
    return pl.pallas_call(
        make_kernel,
        grid=(FF // COLS,),
        in_specs=[pl.BlockSpec(memory_space=pltpu.SMEM)],
        out_specs=[spec, spec],
        out_shape=[jax.ShapeDtypeStruct((D, FF), jnp.bfloat16)] * 2,
        scratch_shapes=[pltpu.VMEM((ROWS, COLS), jnp.int32)],
        compiler_params=pltpu.CompilerParams(vmem_limit_bytes=48 << 20),
        cost_estimate=pl.CostEstimate(flops=2 * D * FF * 600, bytes_accessed=4 * D * FF, transcendentals=0),
    )(seeds)


def activation(gate_part, up_part, share):
    g = gate_part * SCALE_IN
    return (g / (1.0 + jnp.exp(-g)) * (up_part * SCALE_IN) * share).astype(jnp.bfloat16)


def up_kernel(seeds, x, share, act, lin, gate_acc, up_acc):
    expert = pl.program_id(0)
    tile = pl.program_id(1)

    @pl.when((expert == 0) & (tile == 0))
    def _():
        fill_index(lin, FF)

    gate_acc[...] = jnp.zeros_like(gate_acc)
    up_acc[...] = jnp.zeros_like(up_acc)
    seed = seeds[expert + 1]

    @pl.loop(0, D // ROWS)
    def _(step):
        x_part = x[0, :, pl.ds(pl.multiple_of(step * ROWS, ROWS), ROWS)]
        for salt, acc in ((salt_gate, gate_acc), (salt_up, up_acc)):
            w = centred(lin[...] + offset(seed, salt, step * ROWS, tile * COLS, FF))
            acc[...] += jnp.dot(x_part, w, preferred_element_type=jnp.float32)

    act[0] = activation(gate_acc[...], up_acc[...], share[0])


def run_up(seeds, x, share):
    experts, slots, width = x.shape
    return pl.pallas_call(
        up_kernel,
        grid=(experts, FF // COLS),
        in_specs=[
            pl.BlockSpec(memory_space=pltpu.SMEM),
            pl.BlockSpec((1, slots, width), lambda e, t: (e, 0, 0)),
            pl.BlockSpec((1, slots, 1), lambda e, t: (e, 0, 0)),
        ],
        out_specs=pl.BlockSpec((1, slots, COLS), lambda e, t: (e, 0, t)),
        out_shape=jax.ShapeDtypeStruct((experts, slots, FF), jnp.bfloat16),
        scratch_shapes=[
            pltpu.VMEM((ROWS, COLS), jnp.int32),
            pltpu.VMEM((slots, COLS), jnp.float32),
            pltpu.VMEM((slots, COLS), jnp.float32),
        ],
        compiler_params=pltpu.CompilerParams(vmem_limit_bytes=48 << 20),
        cost_estimate=pl.CostEstimate(
            flops=experts * 2 * D * FF * 600, bytes_accessed=2 * x.size, transcendentals=0
        ),
    )(seeds, x, share)


def down_kernel(first, seeds, act, place, out, lin, y):
    tile = pl.program_id(0)
    experts, slots, _ = act.shape

    @pl.when(tile == 0)
    def _():
        fill_index(lin, D)

    col = first + tile * DOWN_COLS

    @pl.loop(0, experts)
    def _(expert):
        seed = seeds[expert]
        total = jnp.zeros((slots, DOWN_COLS), jnp.float32)
        for step in range(FF // ROWS):
            w = centred(lin[...] + offset(seed, salt_down, step * ROWS, col, D))
            total += jnp.dot(
                act[expert, :, step * ROWS : (step + 1) * ROWS], w, preferred_element_type=jnp.float32
            )
        rows = pl.ds(pl.multiple_of(expert * slots, slots), slots)
        y[rows, :] = (total * SCALE_OUT).astype(jnp.bfloat16)

    out[...] = jnp.dot(place[...], y[...], preferred_element_type=jnp.float32).astype(jnp.bfloat16)


def run_down(seeds, act, place, first, columns):
    experts, slots, _ = act.shape
    tokens = place.shape[0]
    return pl.pallas_call(
        functools.partial(down_kernel, first),
        grid=(columns // DOWN_COLS,),
        in_specs=[
            pl.BlockSpec(memory_space=pltpu.SMEM),
            pl.BlockSpec(act.shape, lambda t: (0, 0, 0)),
            pl.BlockSpec(place.shape, lambda t: (0, 0)),
        ],
        out_specs=pl.BlockSpec((tokens, DOWN_COLS), lambda t: (0, t)),
        out_shape=jax.ShapeDtypeStruct((tokens, columns), jnp.bfloat16),
        scratch_shapes=[
            pltpu.VMEM((ROWS, DOWN_COLS), jnp.int32),
            pltpu.VMEM((experts * slots, DOWN_COLS), jnp.bfloat16),
        ],
        compiler_params=pltpu.CompilerParams(vmem_limit_bytes=48 << 20),
        cost_estimate=pl.CostEstimate(
            flops=experts * 2 * columns * FF * 600, bytes_accessed=2 * tokens * columns, transcendentals=0
        ),
    )(seeds, act, place)


def routing(meta, first_expert, group_size, capacity, tok_dev):
    total = meta.shape[0]
    sources = total // tok_dev
    ids, levels, groups = meta[:, :TOP], meta[:, TOP : 2 * TOP], meta[:, 2 * TOP :]
    in_group = jnp.any((ids // group_size)[:, :, None] == groups[:, None, :], axis=2)
    levels = levels.astype(jnp.float32)
    gate = (
        route_scale * levels * in_group.astype(jnp.float32) / jnp.sum(levels, axis=1, keepdims=True)
    )
    mine = first_expert + jnp.arange(EXP_DEV, dtype=jnp.int32)
    chosen = (ids[:, :, None] == mine) & in_group[:, :, None]
    hit = jnp.any(chosen, axis=1)
    share = jnp.sum(jnp.where(chosen, gate[:, :, None], 0.0), axis=1)
    earlier = jnp.tril(jnp.ones((tok_dev, tok_dev), jnp.bfloat16), -1)
    rank = jnp.einsum(
        "ts,bse->bte",
        earlier,
        hit.astype(jnp.bfloat16).reshape(sources, tok_dev, EXP_DEV),
        preferred_element_type=jnp.float32,
    ).reshape(total, EXP_DEV).astype(jnp.int32)
    source = (jnp.arange(total, dtype=jnp.int32) // tok_dev)[:, None]
    slot = jnp.where(hit & (rank < capacity), source * capacity + rank, -1)
    slots = jnp.arange(sources * capacity, dtype=jnp.int32)
    place = (slot[:, :, None] == slots).astype(jnp.bfloat16).reshape(total, -1)
    pick = slot.T[:, None, :] == slots[None, :, None]
    slot_share = jnp.sum(jnp.where(pick, share.T[:, None, :], 0.0), axis=2, keepdims=True)
    return pick.astype(jnp.bfloat16), place, slot_share


def on_device(tokens, expert_ids, node_groups, gate_levels, expert_seeds):
    tok_dev, width = tokens.shape
    devices_all = lax.axis_size(AXES)
    local_count = lax.axis_size("local")
    experts_total = EXP_DEV * devices_all
    capacity = max(2, tok_dev * TOP // experts_total)
    me = lax.axis_index("node") * local_count + lax.axis_index("local")

    meta = jnp.concatenate([expert_ids, gate_levels, node_groups], axis=1)
    meta = lax.all_gather(meta, AXES, axis=0, tiled=True)
    every = lax.all_gather(tokens, AXES, axis=0, tiled=True)
    pick, place, share = routing(meta, me * EXP_DEV, EXP_DEV * local_count, capacity, tok_dev)
    gate_w, up_w = make_weights(expert_seeds)

    slots = pick.shape[1]
    x = jnp.dot(
        pick.reshape(EXP_DEV * slots, -1), every, preferred_element_type=jnp.float32
    ).astype(jnp.bfloat16).reshape(EXP_DEV, slots, width)
    first_act = activation(
        jnp.dot(x[0], gate_w, preferred_element_type=jnp.float32),
        jnp.dot(x[0], up_w, preferred_element_type=jnp.float32),
        share[0],
    )
    act = jnp.concatenate([first_act[None], run_up(expert_seeds, x[1:], share[1:])], axis=0)

    columns = width // CHUNKS
    parts = []
    for chunk in range(CHUNKS):
        partial = run_down(expert_seeds, act, place, chunk * columns, columns)
        parts.append(lax.psum_scatter(partial, AXES, scatter_dimension=0, tiled=True))
    return jnp.concatenate(parts, axis=1)


def solution(mesh):
    rows = P(("rep", "node", "local"), None)
    return jax.shard_map(
        on_device,
        mesh=mesh,
        in_specs=(rows, rows, rows, rows, P(AXES)),
        out_specs=rows,
        check_vma=False,
    )
```

time: 501 us -> 395 us (0.79)
  matrix products: 247 us -> 21.1 us
  Pallas kernels: 0 us -> 222 us
  waiting for transfers between devices: 164 us -> 109 us
  local copies, waits for them, and re-layouts: 61.1 us -> 7.97 us
  blocking collectives: 0 us -> 17.9 us
  between operations: 0.33 us -> 13.3 us
  starting transfers between devices: 10.6 us -> 0.17 us
  loops' own time: 8.94 us -> 0 us
    dot_general x13 -> x4, matrix products: 247 us -> 21.1 us  [the longest x1 9.17 us: on_device(): jnp.dot(pick.reshape(EXP_DEV * slots, -1), every, preferred_element_type=...]
    pallas_call x0 -> x6, Pallas kernels: none -> 222 us  [the longest x1 108 us: run_up(): pl.pallas_call(up_kernel, grid=(experts, FF // COLS), in_specs=[pl.BlockS...]
    all_to_all x2 -> x0, waiting for transfers between devices: 164 us -> none  [the longest x1 82.3 us: on_device(): lax.all_to_all(send_rows, ('node', 'local'), split_axis=0, concat_axis=2,...]
    reduce_scatter x0 -> x4, waiting for transfers between devices: none -> 105 us  [on_device(): lax.psum_scatter(partial, AXES, scatter_dimension=0, tiled=True)]
    gather x2 -> x0, local copies, waits for them, and re-layouts: 25.1 us -> none  [the longest x1 18.1 us: combine_rows(): picked = padded[slot_index]]
    all_gather x0 -> x1, blocking collectives: none -> 17.9 us  [on_device(): meta = lax.all_gather(meta, AXES, axis=0, tiled=True)]
    all_to_all x2 -> x0, local copies, waits for them, and re-layouts: 12.3 us -> none  [the longest x1 6.82 us: on_device(): lax.all_to_all(send_rows, ('node', 'local'), split_axis=0, concat_axis=2,...]
    while x1 -> x0, local copies, waits for them, and re-layouts: 11.7 us -> none  [run_experts(): lax.scan(per_expert, jnp.zeros((), jnp.int32), (local_seeds, expert_rows))]
  transfers between devices with their start and end apart: 2 -> 5, of which waited for: 2 -> 4; matrix products, arithmetic and copies ran while one was open for 0% -> 1% of each run, Pallas kernels for 0% -> 24%
where the time goes in v1:
time: 395 us
  Pallas kernels  222 us (56%)
  waiting for transfers between devices  109 us (28%)
  matrix products  21.1 us (5%)
  blocking collectives  17.9 us (5%)
  between operations  13.3 us (3%)
  local copies, waits for them, and re-layouts  7.97 us (2%)
    pallas_call x1, Pallas kernels, run_up(): pl.pallas_call(up_kernel, grid=(experts, FF // COLS), in_specs=[pl.BlockS...  108 us
    reduce_scatter x4, waiting for transfers between devices, on_device(): lax.psum_scatter(partial, AXES, scatter_dimension=0, tiled=True)  105 us
    pallas_call x4, Pallas kernels, run_down(): pl.pallas_call(functools.partial(down_kernel, first), grid=(columns // DO...  84.6 us
    pallas_call x1, Pallas kernels, make_weights(): pl.pallas_call(make_kernel, grid=(FF // COLS,), in_specs=[pl.BlockSpec(me...  29.9 us
    all_gather x1, blocking collectives, on_device(): meta = lax.all_gather(meta, AXES, axis=0, tiled=True)  17.9 us
    dot_general x1, matrix products, on_device(): jnp.dot(pick.reshape(EXP_DEV * slots, -1), every, preferred_element_type=...  9.17 us
    dot_general x1, matrix products, on_device(): jnp.dot(x[0], up_w, preferred_element_type=jnp.float32)  7.91 us
  transfers between devices with their start and end apart: 5, of which 4 were waited for; matrix products, arithmetic and copies ran while one was open for 1% of the time, Pallas kernels for 24%

profile of v1, /device:TPU:0, one launch (start us, length us, event | category | flops | bytes accessed | tf_op | source)
XLA Modules:
  0.0 395.0 jit_solution(6739504832866811234)
XLA Ops:
  6.5 0.0 all-gather.3.cloned.1.call-start
  6.5 0.7 all-gather.3.cloned.1.call-update
  7.3 0.0 reduce-scatter.5.cloned.1.call-start
  7.3 0.7 add_bitcast_fusion
  8.0 17.9 %all-gather = s32[8,64,18]{1,2,0:T(8,128)S(1)} all-gather(s32[1,64,18]{1,2,0:T(8,128)S(1)} %add_bitcast_fusion), channel_id=1, replica_groups=mesh['rep'=4,'node'=4,'local'=2] {'node','local'}, dimensions={0}, use_global_device_ids=true | all-gather | bytes 41472 | tf_op jit(solution)/shard_map/all_gather | solution.py:222
  26.0 0.1 reshape.73
  26.1 0.1 fusion.24
  26.2 0.1 reshape.71
  26.3 0.2 fusion.22
  26.5 0.1 convert_element_type.31
  26.6 0.1 copy.25
  26.8 0.1 select_reduce_fusion.1
  26.9 0.2 select_reduce_fusion
  27.1 0.1 copy.24.share
  27.3 1.3 eq.84
  28.6 0.3 fusion.23
  28.9 0.0 copy-start
  29.0 0.6 copy-done
  29.6 29.9 %shard_map.55 = (bf16[7168,1024]{1,0:T(8,128)(2,1)}, bf16[7168,1024]{1,0:T(8,128)(2,1)}) custom-call(s32[4]{0:T(128)S(1)} %copy-done), custom_call_target="tpu_custom_call" | custom-call | flops 8808038400 | bytes 29360128 | tf_op jit(solution)/shard_map/pallas_call | solution.py:72
  59.5 2.6 all-gather.3.cloned.1.call-done
  62.1 0.0 slice-start
  62.1 0.0 slice-start.1
  62.1 0.0 slice-start.2
  62.1 9.2 %convolution_convert_fusion = bf16[512,7168]{1,0:T(8,128)(2,1)} fusion(pred[512,512]{1,0:T(32,128)(4,1)S(1)} %get-tuple-element.12, bf16[512,7168]{1,0:T(8,128)(2,1)} %all-gather.3.cloned.1.call-done), kind=kOutput, calls=%fused_computation | convolution fusion | flops 3761766400 | bytes 14942208 | tf_op jit(solution)/shard_map/dot_general | solution.py:228
  71.3 0.0 slice-start.3
  71.3 5.4 %slice.43 = bf16[384,7168]{1,0:T(8,128)(2,1)} slice(bf16[512,7168]{1,0:T(8,128)(2,1)} %convolution_convert_fusion), slice={[128:512], [0:7168]} | slice | bytes 11010048 | tf_op jit(solution)/shard_map/slice | solution.py:236
  76.7 0.0 slice-done
  76.7 0.0 slice-done.1
  76.7 0.0 slice-done.2
  76.7 0.0 slice-done.3
  76.7 3.8 fusion.4
  80.5 107.6 %shard_map.56 = bf16[3,128,1024]{2,1,0:T(8,128)(2,1)S(1)} custom-call(s32[4]{0:T(128)S(1)} %copy-done, bf16[3,128,7168]{2,1,0:T(8,128)(2,1)} %bitcast.38, f32[3,128,1]{2,1,0:T(8,128)S(1)} %copy.24.share), custom_call_target="tpu_custom_call" | custom-call | flops 26424115200 | bytes 5505024 | tf_op jit(solution)/shard_map/pallas_call | solution.py:113
  188.1 0.0 copy-start.1
  188.1 7.9 %fusion.19 = bf16[1,128,1024]{2,1,0:T(8,128)(2,1)S(1)} fusion(bf16[7168,1024]{1,0:T(8,128)(2,1)} %get-tuple-element.8, bf16[512,7168]{1,0:T(8,128)(2,1)} %convolution_convert_fusion, f32[128,1024]{1,0:T(8,128)S(1)} %fusion.4, f32[128]{0:T(128)S(1)} %slice_bitcast_fusion.1), kind=kOutput, calls=%fused_computation.10 | convolution fusion | flops 1879965696 | bytes 17302016 | tf_op jit(solution)/shard_map/dot_general | solution.py:233
  196.0 0.1 pad_maximum_fusion.act
  196.1 0.0 copy-done.1
  196.1 21.2 %shard_map.57 = bf16[512,1792]{1,0:T(8,128)(2,1)} custom-call(s32[4]{0:T(128)S(1)} %copy-done.1, bf16[4,128,1024]{2,1,0:T(8,128)(2,1)S(1)} %pad_maximum_fusion.act, bf16[512,512]{1,0:T(8,128)(2,1)S(1)} %get-tuple-element.11.place), custom_call_target="tpu_custom_call" | custom-call | flops 8808038400 | bytes 1835008 | tf_op jit(solution)/shard_map/pallas_call | solution.py:163
  217.3 0.0 reduce-scatter.5.cloned.1.call-update
  217.3 0.0 reduce-scatter.7.cloned.1.call-start
  217.4 21.1 %shard_map.58 = bf16[512,1792]{1,0:T(8,128)(2,1)} custom-call(s32[4]{0:T(128)S(1)} %copy-done.1, bf16[4,128,1024]{2,1,0:T(8,128)(2,1)S(1)} %pad_maximum_fusion.act, bf16[512,512]{1,0:T(8,128)(2,1)S(1)} %get-tuple-element.11.place), custom_call_target="tpu_custom_call" | custom-call | flops 8808038400 | bytes 1835008 | tf_op jit(solution)/shard_map/pallas_call | solution.py:163
  238.5 0.0 reduce-scatter.7.cloned.1.call-update
  238.6 0.0 reduce-scatter.9.cloned.1.call-start
  238.6 21.1 %shard_map.59 = bf16[512,1792]{1,0:T(8,128)(2,1)} custom-call(s32[4]{0:T(128)S(1)} %copy-done.1, bf16[4,128,1024]{2,1,0:T(8,128)(2,1)S(1)} %pad_maximum_fusion.act, bf16[512,512]{1,0:T(8,128)(2,1)S(1)} %get-tuple-element.11.place), custom_call_target="tpu_custom_call" | custom-call | flops 8808038400 | bytes 1835008 | tf_op jit(solution)/shard_map/pallas_call | solution.py:163
  259.8 0.0 reduce-scatter.9.cloned.1.call-update
  259.8 0.0 reduce-scatter.11.cloned.1.call-start
  259.8 21.2 %shard_map.60 = bf16[512,1792]{1,0:T(8,128)(2,1)} custom-call(s32[4]{0:T(128)S(1)} %copy-done.1, bf16[4,128,1024]{2,1,0:T(8,128)(2,1)S(1)} %pad_maximum_fusion.act, bf16[512,512]{1,0:T(8,128)(2,1)S(1)} %get-tuple-element.11.place), custom_call_target="tpu_custom_call" | custom-call | flops 8808038400 | bytes 1835008 | tf_op jit(solution)/shard_map/pallas_call | solution.py:163
  281.0 0.0 reduce-scatter.11.cloned.1.call-update
  281.0 0.0 reduce-scatter.5.cloned.1.call-done
  281.1 19.4 %reduce-scatter.7.cloned.1.call-done = bf16[64,1792]{1,0:T(8,128)(2,1)} async-done(((bf16[512,1792]{1,0:T(8,128)(2,1)}), bf16[64,1792]{1,0:T(8,128)(2,1)}) %reduce-scatter.7.cloned.1.call-update) | async-done | bytes 229392 | tf_op jit(solution)/shard_map/reduce_scatter | solution.py:242
  300.4 42.9 %reduce-scatter.9.cloned.1.call-done = bf16[64,1792]{1,0:T(8,128)(2,1)} async-done(((bf16[512,1792]{1,0:T(8,128)(2,1)}), bf16[64,1792]{1,0:T(8,128)(2,1)}) %reduce-scatter.9.cloned.1.call-update) | async-done | bytes 229392 | tf_op jit(solution)/shard_map/reduce_scatter | solution.py:242
  343.3 42.9 %reduce-scatter.11.cloned.1.call-done = bf16[64,1792]{1,0:T(8,128)(2,1)} async-done(((bf16[512,1792]{1,0:T(8,128)(2,1)}), bf16[64,1792]{1,0:T(8,128)(2,1)}) %reduce-scatter.11.cloned.1.call-update) | async-done | bytes 229392 | tf_op jit(solution)/shard_map/reduce_scatter | solution.py:242
  386.3 2.3 pad_maximum_fusion.1
  (14 shorter events, 0.1 us)
Async XLA Ops:
  6.5 55.6 %all-gather.3.cloned.1.call-start = ((), (), s32[]{:S(2)}) async-start(), calls=%async_computation.4 | async-start | bytes 8257536 | tf_op jit(solution)/shard_map/all_gather | solution.py:223
  7.3 273.8 %reduce-scatter.5.cloned.1.call-start = ((), (), s32[]{:S(2)}) async-start(), calls=%async_computation.5 | async-start | bytes 2064384 | tf_op jit(solution)/shard_map/reduce_scatter | solution.py:242
  28.9 0.7 copy-start
  62.1 14.6 %slice-start = ((s8[14680064]{0:T(1024)(128)(4,1)}), s8[4194304]{0:T(1024)(128)(4,1)S(1)}, s32[]{:S(2)}) async-start(s8[14680064]{0:T(1024)(128)(4,1)} %bitcast.36), calls=%async_computation.9 | async-start | bytes 8388608
  62.1 14.6 %slice-start.1 = ((s8[14680064]{0:T(1024)(128)(4,1)}), s8[4194304]{0:T(1024)(128)(4,1)S(1)}, s32[]{:S(2)}) async-start(s8[14680064]{0:T(1024)(128)(4,1)} %bitcast.36), calls=%async_computation.10 | async-start | bytes 8388608
  62.1 14.6 %slice-start.2 = ((s8[14680064]{0:T(1024)(128)(4,1)}), s8[4194304]{0:T(1024)(128)(4,1)S(1)}, s32[]{:S(2)}) async-start(s8[14680064]{0:T(1024)(128)(4,1)} %bitcast.36), calls=%async_computation.11 | async-start | bytes 8388608
  71.3 5.4 %slice-start.3 = ((s8[14680064]{0:T(1024)(128)(4,1)}), s8[2097152]{0:T(1024)(128)(4,1)S(1)}, s32[]{:S(2)}) async-start(s8[14680064]{0:T(1024)(128)(4,1)} %bitcast.36), calls=%async_computation.12 | async-start | bytes 4194304
  188.1 8.0 %copy-start.1 = (s32[4]{0:T(128)S(1)}, s32[4]{0:T(128)}, u32[]{:S(2)}) copy-start(s32[4]{0:T(128)} %seeds.11) | copy-start | bytes 52
  217.3 83.1 %reduce-scatter.7.cloned.1.call-start = ((), (), s32[]{:S(2)}) async-start(), calls=%async_computation.6 | async-start | bytes 2064384 | tf_op jit(solution)/shard_map/reduce_scatter | solution.py:242
  238.6 104.8 %reduce-scatter.9.cloned.1.call-start = ((), (), s32[]{:S(2)}) async-start(), calls=%async_computation.7 | async-start | bytes 2064384 | tf_op jit(solution)/shard_map/reduce_scatter | solution.py:242
  259.8 126.5 %reduce-scatter.11.cloned.1.call-start = ((), (), s32[]{:S(2)}) async-start(), calls=%async_computation.8 | async-start | bytes 2064384 | tf_op jit(solution)/shard_map/reduce_scatter | solution.py:242
Sparse Core Ops, SparseCore 0:
  9.2 52.8 all-gather.2
  217.5 39.7 reduce-scatter.4
  260.7 39.7 reduce-scatter.6
  303.6 39.6 reduce-scatter.8
  346.6 39.6 reduce-scatter.10

commit v2 on v1

v2 whole, which is shorter than its diff:
```python
import functools
import math

import jax
import jax.numpy as jnp
from jax import lax
from jax.experimental import pallas as pl
from jax.experimental.pallas import tpu as pltpu
from jax.sharding import PartitionSpec as P

D = 7168
FF = 1024
TOP = 8
EXP_DEV = 4
AXES = ("node", "local")

route_scale = 2.5
salt_gate = 1013904223
salt_up = 1664525
salt_down = 22695477
INDEX_MUL = 747796405
SEED_MUL = 1103515245
SCALE_IN = math.sqrt(3.0 / D) / 32768.0
SCALE_OUT = math.sqrt(3.0 / FF) / 32768.0

ROWS = 512
COLS = 256
DOWN_ROWS = 256
DOWN_COLS = 512
AHEAD = 2
META = 128


def as_int32(value):
    return jnp.int32((value + 2**31) % 2**32 - 2**31)


def centred(hashed):
    hashed = hashed ^ (hashed >> 15)
    hashed = hashed * jnp.int32(277803737)
    hashed = hashed ^ (hashed >> 13)
    hashed = hashed * jnp.int32(668265263)
    hashed = hashed ^ (hashed >> 16)
    sixteen = (hashed >> 8) & jnp.int32(65535)
    return (sixteen.astype(jnp.float32) - 32767.5).astype(jnp.bfloat16)


def fill_index(lin, columns):
    row = lax.broadcasted_iota(jnp.int32, lin.shape, 0)
    col = lax.broadcasted_iota(jnp.int32, lin.shape, 1)
    lin[...] = (row * columns + col) * as_int32(INDEX_MUL)


def offset(seed, salt, row, col, columns):
    return (row * columns + col) * as_int32(INDEX_MUL) + seed * as_int32(SEED_MUL) + jnp.int32(salt)


def make_kernel(seeds, gate_out, up_out, lin):
    expert = pl.program_id(0)
    tile = pl.program_id(1)

    @pl.when((expert == 0) & (tile == 0))
    def _():
        fill_index(lin, FF)

    seed = seeds[EXP_DEV - AHEAD + expert]

    @pl.loop(0, D // ROWS)
    def _(step):
        rows = pl.ds(pl.multiple_of(step * ROWS, ROWS), ROWS)
        for salt, out in ((salt_gate, gate_out), (salt_up, up_out)):
            out[0, rows, :] = centred(lin[...] + offset(seed, salt, step * ROWS, tile * COLS, FF))


def make_weights(seeds):
    spec = pl.BlockSpec((1, D, COLS), lambda e, t: (e, 0, t))
    return pl.pallas_call(
        make_kernel,
        grid=(AHEAD, FF // COLS),
        in_specs=[pl.BlockSpec(memory_space=pltpu.SMEM)],
        out_specs=[spec, spec],
        out_shape=[jax.ShapeDtypeStruct((AHEAD, D, FF), jnp.bfloat16)] * 2,
        scratch_shapes=[pltpu.VMEM((ROWS, COLS), jnp.int32)],
        compiler_params=pltpu.CompilerParams(vmem_limit_bytes=48 << 20),
        cost_estimate=pl.CostEstimate(
            flops=AHEAD * 2 * D * FF * 600, bytes_accessed=AHEAD * 4 * D * FF, transcendentals=0
        ),
    )(seeds)


def activation(gate_part, up_part, share):
    g = gate_part * SCALE_IN
    return (g / (1.0 + jnp.exp(-g)) * (up_part * SCALE_IN) * share).astype(jnp.bfloat16)


def up_kernel(seeds, x, share, gate_w, up_w, act, lin, acc):
    expert = pl.program_id(0)
    tile = pl.program_id(1)

    @pl.when((expert == 0) & (tile == 0))
    def _():
        fill_index(lin, FF)

    acc[...] = jnp.zeros_like(acc)
    seed = seeds[expert]

    @pl.loop(0, D // ROWS, unroll=2)
    def _(step):
        rows = pl.ds(pl.multiple_of(step * ROWS, ROWS), ROWS)
        hashed_x, ready_x = x[0, 0, :, rows], x[1, 0, :, rows]
        for which, (salt, ready) in enumerate(((salt_gate, gate_w), (salt_up, up_w))):
            w = centred(lin[...] + offset(seed, salt, step * ROWS, tile * COLS, FF))
            acc[2 + which] += jnp.dot(ready_x, ready[0, rows, :], preferred_element_type=jnp.float32)
            acc[which] += jnp.dot(hashed_x, w, preferred_element_type=jnp.float32)

    act[0, 0] = activation(acc[0], acc[1], share[0, 0])
    act[1, 0] = activation(acc[2], acc[3], share[1, 0])


def run_up(seeds, x, share, gate_w, up_w):
    experts, slots, _ = x.shape
    half = experts - AHEAD
    x = x.reshape(2, half, slots, -1)
    share = share.reshape(2, half, slots, 1)
    weights = pl.BlockSpec((1, D, COLS), lambda e, t: (e, 0, t))
    return pl.pallas_call(
        up_kernel,
        grid=(half, FF // COLS),
        in_specs=[
            pl.BlockSpec(memory_space=pltpu.SMEM),
            pl.BlockSpec((2, 1, slots, D), lambda e, t: (0, e, 0, 0)),
            pl.BlockSpec((2, 1, slots, 1), lambda e, t: (0, e, 0, 0)),
            weights,
            weights,
        ],
        out_specs=pl.BlockSpec((2, 1, slots, COLS), lambda e, t: (0, e, 0, t)),
        out_shape=jax.ShapeDtypeStruct((2, half, slots, FF), jnp.bfloat16),
        scratch_shapes=[
            pltpu.VMEM((ROWS, COLS), jnp.int32),
            pltpu.VMEM((4, slots, COLS), jnp.float32),
        ],
        compiler_params=pltpu.CompilerParams(vmem_limit_bytes=48 << 20),
        cost_estimate=pl.CostEstimate(
            flops=half * 2 * D * FF * 600, bytes_accessed=2 * x.size, transcendentals=0
        ),
    )(seeds, x, share, gate_w, up_w).reshape(experts, slots, FF)


def down_kernel(devices, local_count, seeds, act, place, out, lin, y, sent, arrived, send_sem, recv_sem):
    tile = pl.program_id(0)
    tiles = pl.num_programs(0)
    experts, slots, _ = act.shape
    tok_dev, width = out.shape
    me = lax.axis_index("node") * local_count + lax.axis_index("local")
    slot = lax.rem(tile, 2)

    def peer(step):
        return lax.rem(me + step, devices)

    def device(index):
        return {"node": index // local_count, "local": lax.rem(index, local_count)}

    barrier = pltpu.get_barrier_semaphore()

    @pl.when(tile == 0)
    def _():
        @pl.loop(1, devices)
        def _(step):
            pl.semaphore_signal(
                barrier, inc=1, device_id=device(peer(step)), device_id_type=pl.DeviceIdType.MESH
            )

        fill_index(lin, D)

    for expert in range(experts):
        total = jnp.zeros((slots, DOWN_COLS), jnp.float32)
        for step in range(FF // DOWN_ROWS):
            w = centred(
                lin[...] + offset(seeds[expert], salt_down, step * DOWN_ROWS, tile * DOWN_COLS, D)
            )
            total += jnp.dot(
                act[expert, :, step * DOWN_ROWS : (step + 1) * DOWN_ROWS],
                w,
                preferred_element_type=jnp.float32,
            )
        y[expert * slots : (expert + 1) * slots, :] = (total * SCALE_OUT).astype(jnp.bfloat16)

    def copy(step, where, column):
        to = peer(step)
        return pltpu.make_async_remote_copy(
            src_ref=sent.at[where, pl.ds(pl.multiple_of(to * tok_dev, tok_dev), tok_dev), :],
            dst_ref=arrived.at[me, :, pl.ds(pl.multiple_of(column * DOWN_COLS, DOWN_COLS), DOWN_COLS)],
            send_sem=send_sem.at[where, to],
            recv_sem=recv_sem.at[me],
            device_id=device(to),
            device_id_type=pl.DeviceIdType.MESH,
        )

    @pl.when(tile == 0)
    def _():
        pl.semaphore_wait(barrier, devices - 1)

    @pl.when(tile >= 2)
    def _():
        @pl.loop(1, devices)
        def _(step):
            copy(step, slot, tile - 2).wait_send()

    sent[slot] = jnp.dot(place[...], y[...], preferred_element_type=jnp.float32).astype(jnp.bfloat16)

    @pl.loop(1, devices)
    def _(step):
        copy(step, slot, tile).start()

    own = pl.ds(pl.multiple_of(me * tok_dev, tok_dev), tok_dev)
    columns = pl.ds(pl.multiple_of(tile * DOWN_COLS, DOWN_COLS), DOWN_COLS)
    arrived[me, :, columns] = sent[slot, own, :]

    @pl.when(tile == tiles - 1)
    def _():
        @pl.loop(1, devices)
        def _(step):
            copy(step, 1 - slot, tile - 1).wait_send()
            copy(step, slot, tile).wait_send()
            source = peer(step)
            pltpu.make_async_remote_copy(
                src_ref=arrived.at[source],
                dst_ref=arrived.at[source],
                send_sem=send_sem.at[0, source],
                recv_sem=recv_sem.at[source],
                device_id=device(source),
                device_id_type=pl.DeviceIdType.MESH,
            ).wait_recv()

        @pl.loop(0, width // DOWN_COLS)
        def _(part):
            span = pl.ds(pl.multiple_of(part * DOWN_COLS, DOWN_COLS), DOWN_COLS)

            def add(source, total):
                return total + arrived[source, :, span].astype(jnp.float32)

            total = lax.fori_loop(0, devices, add, jnp.zeros((tok_dev, DOWN_COLS), jnp.float32))
            out[:, span] = total.astype(jnp.bfloat16)


def run_down(seeds, act, place, tok_dev, width, devices, local_count):
    experts, slots, _ = act.shape
    tokens = place.shape[0]
    return pl.pallas_call(
        functools.partial(down_kernel, devices, local_count),
        grid=(width // DOWN_COLS,),
        in_specs=[
            pl.BlockSpec(memory_space=pltpu.SMEM),
            pl.BlockSpec(act.shape, lambda t: (0, 0, 0)),
            pl.BlockSpec(place.shape, lambda t: (0, 0)),
        ],
        out_specs=pl.BlockSpec((tok_dev, width), lambda t: (0, 0)),
        out_shape=jax.ShapeDtypeStruct((tok_dev, width), jnp.bfloat16),
        scratch_shapes=[
            pltpu.VMEM((DOWN_ROWS, DOWN_COLS), jnp.int32),
            pltpu.VMEM((experts * slots, DOWN_COLS), jnp.bfloat16),
            pltpu.VMEM((2, tokens, DOWN_COLS), jnp.bfloat16),
            pltpu.VMEM((devices, tok_dev, width), jnp.bfloat16),
            pltpu.SemaphoreType.DMA((2, devices)),
            pltpu.SemaphoreType.DMA((devices,)),
        ],
        compiler_params=pltpu.CompilerParams(
            vmem_limit_bytes=56 << 20, collective_id=0, has_side_effects=True
        ),
        cost_estimate=pl.CostEstimate(
            flops=experts * 2 * width * FF * 600, bytes_accessed=2 * tokens * width, transcendentals=0
        ),
    )(seeds, act, place)


def routing(meta, first_expert, group_size, capacity, tok_dev):
    total = meta.shape[0]
    sources = total // tok_dev
    ids, levels, groups = meta[:, :TOP], meta[:, TOP : 2 * TOP], meta[:, 2 * TOP :]
    in_group = jnp.any((ids // group_size)[:, :, None] == groups[:, None, :], axis=2)
    levels = levels.astype(jnp.float32)
    gate = (
        route_scale * levels * in_group.astype(jnp.float32) / jnp.sum(levels, axis=1, keepdims=True)
    )
    mine = first_expert + jnp.arange(EXP_DEV, dtype=jnp.int32)
    chosen = (ids[:, :, None] == mine) & in_group[:, :, None]
    hit = jnp.any(chosen, axis=1)
    share = jnp.sum(jnp.where(chosen, gate[:, :, None], 0.0), axis=1)
    earlier = jnp.tril(jnp.ones((tok_dev, tok_dev), jnp.bfloat16), -1)
    rank = jnp.einsum(
        "ts,bse->bte",
        earlier,
        hit.astype(jnp.bfloat16).reshape(sources, tok_dev, EXP_DEV),
        preferred_element_type=jnp.float32,
    ).reshape(total, EXP_DEV).astype(jnp.int32)
    source = (jnp.arange(total, dtype=jnp.int32) // tok_dev)[:, None]
    slot = jnp.where(hit & (rank < capacity), source * capacity + rank, -1)
    slots = jnp.arange(sources * capacity, dtype=jnp.int32)
    place = (slot[:, :, None] == slots).astype(jnp.bfloat16).reshape(total, -1)
    pick = slot.T[:, None, :] == slots[None, :, None]
    slot_share = jnp.sum(jnp.where(pick, share.T[:, None, :], 0.0), axis=2, keepdims=True)
    return pick.astype(jnp.bfloat16), place, slot_share


def on_device(tokens, expert_ids, node_groups, gate_levels, expert_seeds):
    tok_dev, width = tokens.shape
    devices_all = lax.axis_size(AXES)
    local_count = lax.axis_size("local")
    experts_total = EXP_DEV * devices_all
    capacity = max(2, tok_dev * TOP // experts_total)
    me = lax.axis_index("node") * local_count + lax.axis_index("local")

    meta = jnp.concatenate([expert_ids, gate_levels, node_groups], axis=1).astype(jnp.bfloat16)
    meta = jnp.pad(meta, ((0, 0), (0, META - meta.shape[1])))
    every = lax.all_gather(jnp.concatenate([tokens, meta], axis=1), AXES, axis=0, tiled=True)
    gate_w, up_w = make_weights(expert_seeds)
    pick, place, share = routing(
        every[:, width : width + 2 * TOP + node_groups.shape[1]].astype(jnp.int32),
        me * EXP_DEV,
        EXP_DEV * local_count,
        capacity,
        tok_dev,
    )

    slots = pick.shape[1]
    x = jnp.dot(
        pick.reshape(EXP_DEV * slots, -1), every, preferred_element_type=jnp.float32
    ).astype(jnp.bfloat16).reshape(EXP_DEV, slots, -1)
    act = run_up(expert_seeds, x, share, gate_w, up_w)
    return run_down(expert_seeds, act, place, tok_dev, width, devices_all, local_count)


def solution(mesh):
    rows = P(("rep", "node", "local"), None)
    return jax.shard_map(
        on_device,
        mesh=mesh,
        in_specs=(rows, rows, rows, rows, P(AXES)),
        out_specs=rows,
        check_vma=False,
    )
```

time: 395 us -> 252 us (0.64)
  waiting for transfers between devices: 109 us -> 0.02 us
  blocking collectives: 17.9 us -> 0 us
  matrix products: 21.1 us -> 9.53 us
  Pallas kernels: 222 us -> 216 us
    reduce_scatter x4 -> x0, waiting for transfers between devices: 105 us -> none  [on_device(): lax.psum_scatter(partial, AXES, scatter_dimension=0, tiled=True)]
    all_gather x1 -> x0, blocking collectives: 17.9 us -> none  [on_device(): meta = lax.all_gather(meta, AXES, axis=0, tiled=True)]
    dot_general x2 -> x0, matrix products: 11.7 us -> none  [the longest x1 7.91 us: on_device(): jnp.dot(x[0], up_w, preferred_element_type=jnp.float32)]
    pallas_call x6 -> x3, Pallas kernels: 222 us -> 216 us  [the longest x1 91.8 us: run_down(): pl.pallas_call(functools.partial(down_kernel, devices, local_count), grid...]
    slice x3 -> x1, local copies, waits for them, and re-layouts: 5.57 us -> 0.91 us  [on_device(): every[:, width:width + 2 * TOP + node_groups.shape[1]].astype(jnp.int32)]
  transfers between devices with their start and end apart: 5 -> 1, of which waited for: 4 -> 0; matrix products, arithmetic and copies ran while one was open for 1% -> 0% of each run, Pallas kernels for 24% -> 22%
where the time goes in v2:
time: 252 us
  Pallas kernels  216 us (86%)
  between operations  13.5 us (5%)
  matrix products  9.53 us (4%)
  local copies, waits for them, and re-layouts  6.71 us (3%)
  other arithmetic  5.87 us (2%)
    pallas_call x1, Pallas kernels, run_down(): pl.pallas_call(functools.partial(down_kernel, devices, local_count), grid...  91.8 us
    pallas_call x1, Pallas kernels, run_up(): pl.pallas_call(up_kernel, grid=(half, FF // COLS), in_specs=[pl.BlockSpec...  68.4 us
    pallas_call x1, Pallas kernels, make_weights(): pl.pallas_call(make_kernel, grid=(AHEAD, FF // COLS), in_specs=[pl.BlockS...  56.1 us
    dot_general x1, matrix products, on_device(): jnp.dot(pick.reshape(EXP_DEV * slots, -1), every, preferred_element_type=...  9.33 us
  transfers between devices with their start and end apart: 1, of which 0 were waited for; matrix products, arithmetic and copies ran while one was open for 0% of the time, Pallas kernels for 22%

profile of v2, /device:TPU:0, one launch (start us, length us, event | category | flops | bytes accessed | tf_op | source)
XLA Modules:
  0.0 251.9 jit_solution(12195255373827540150)
XLA Ops:
  6.5 0.0 all-gather.2.cloned.1.call-start
  6.5 0.7 convert.11
  7.2 0.7 convert.9
  7.9 0.7 convert.10
  8.6 0.1 copy.20
  8.7 2.2 fusion.3
  10.9 0.0 all-gather.2.cloned.1.call-update
  11.0 0.0 copy-start.1
  11.0 0.6 copy-done.1
  11.6 56.1 %shard_map.55 = (bf16[2,7168,1024]{2,1,0:T(8,128)(2,1)}, bf16[2,7168,1024]{2,1,0:T(8,128)(2,1)}) custom-call(s32[4]{0:T(128)S(1)} %copy-done.1), custom_call_target="tpu_custom_call" | custom-call | flops 17616076800 | bytes 58720256 | tf_op jit(solution)/shard_map/pallas_call | solution.py:77
  67.7 0.0 all-gather.2.cloned.1.call-done
  67.7 0.9 slice.16
  68.6 0.1 copy.24
  68.8 0.1 fusion.4
  68.9 0.1 select_reduce_fusion.1
  69.0 0.1 reshape.66
  69.1 0.2 fusion.1
  69.3 0.1 convert_element_type.35
  69.4 0.1 copy.23
  69.6 0.2 select_reduce_fusion
  69.8 0.2 copy.22.share
  69.9 1.3 eq.84
  71.3 1.1 fusion.2
  72.4 0.0 copy-start.2
  72.4 9.3 %convolution_convert_fusion = bf16[512,7296]{1,0:T(8,128)(2,1)} fusion(pred[512,512]{1,0:T(32,128)(4,1)S(1)} %get-tuple-element.12, bf16[512,7296]{1,0:T(8,128)(2,1)} %all-gather.2.cloned.1.call-done), kind=kOutput, calls=%fused_computation | convolution fusion | flops 3828940800 | bytes 15204352 | tf_op jit(solution)/shard_map/dot_general | solution.py:326
  81.7 0.0 copy-done.2
  81.7 68.4 %shard_map.56 = bf16[2,2,128,1024]{3,2,1,0:T(8,128)(2,1)S(1)} custom-call(s32[4]{0:T(128)S(1)} %copy-done.2, bf16[2,2,128,7296]{3,2,1,0:T(8,128)(2,1)} %bitcast.27, f32[2,2,128,1]{3,2,1,0:T(8,128)S(1)} %copy.22.share, bf16[2,7168,1024]{2,1,0:T(8,128)(2,1)} %get-tuple-element.7.gate_w, bf16[2,7168,1024]{2,1,0:T(8,128)(2,1)} %get-tuple-element.8.up_w), custom_call_target="tpu_custom_call" | custom-call | flops 17616076800 | bytes 7471104 | tf_op jit(solution)/shard_map/pallas_call | solution.py:126
  150.1 0.0 copy-start
  150.1 1.0 copy-done
  151.1 91.8 %shard_map.57 = bf16[64,7168]{1,0:T(8,128)(2,1)} custom-call(s32[4]{0:T(128)} %seeds.5, bf16[4,128,1024]{2,1,0:T(8,128)(2,1)} %bitcast.26, bf16[512,512]{1,0:T(8,128)(2,1)} %get-tuple-element.11.place), custom_call_target="tpu_custom_call" | custom-call | flops 35232153600 | bytes 7340032 | tf_op jit(solution)/shard_map/pallas_call | solution.py:249
  242.9 2.2 copy.32
  (12 shorter events, 0.1 us)
Async XLA Ops:
  6.5 61.2 %all-gather.2.cloned.1.call-start = ((), (), s32[]{:S(2)}) async-start(), calls=%async_computation | async-start | bytes 8404992 | tf_op jit(solution)/shard_map/all_gather | solution.py:315
  11.0 0.7 copy-start.1
  72.4 9.3 %copy-start.2 = (s32[4]{0:T(128)S(1)}, s32[4]{0:T(128)}, u32[]{:S(2)}) copy-start(s32[4]{0:T(128)} %seeds.5) | copy-start | bytes 52
  150.1 1.0 copy-start
Sparse Core Ops, SparseCore 0:
  11.0 53.2 all-gather.1

commit v3 on v2

--- a/solution.py
+++ b/solution.py
@@ -20,12 +20,12 @@
 salt_down = 22695477
 INDEX_MUL = 747796405
 SEED_MUL = 1103515245
-SCALE_IN = math.sqrt(3.0 / D) / 32768.0
-SCALE_OUT = math.sqrt(3.0 / FF) / 32768.0
+SCALE_IN = math.sqrt(3.0 / D) / 8388608.0
+SCALE_OUT = math.sqrt(3.0 / FF) / 8388608.0
 
 ROWS = 512
 COLS = 256
-DOWN_ROWS = 256
+PIECE = 64
 DOWN_COLS = 512
 AHEAD = 2
 META = 128
@@ -41,8 +41,8 @@
     hashed = hashed ^ (hashed >> 13)
     hashed = hashed * jnp.int32(668265263)
     hashed = hashed ^ (hashed >> 16)
-    sixteen = (hashed >> 8) & jnp.int32(65535)
-    return (sixteen.astype(jnp.float32) - 32767.5).astype(jnp.bfloat16)
+    sixteen = (hashed & jnp.int32(65535 << 8)).astype(jnp.float32)
+    return (sixteen - 32767.5 * 256.0).astype(jnp.bfloat16)
 
 
 def fill_index(lin, columns):
@@ -51,6 +51,12 @@
     lin[...] = (row * columns + col) * as_int32(INDEX_MUL)
 
 
+def hash_rows(out, where, lin, base, rows, columns):
+    for piece in range(0, rows, PIECE):
+        start = base + as_int32(piece * columns * INDEX_MUL)
+        out[(*where, slice(piece, piece + PIECE), slice(None))] = centred(lin[...] + start)
+
+
 def offset(seed, salt, row, col, columns):
     return (row * columns + col) * as_int32(INDEX_MUL) + seed * as_int32(SEED_MUL) + jnp.int32(salt)
 
@@ -69,7 +75,8 @@
     def _(step):
         rows = pl.ds(pl.multiple_of(step * ROWS, ROWS), ROWS)
         for salt, out in ((salt_gate, gate_out), (salt_up, up_out)):
-            out[0, rows, :] = centred(lin[...] + offset(seed, salt, step * ROWS, tile * COLS, FF))
+            base = offset(seed, salt, step * ROWS, tile * COLS, FF)
+            hash_rows(out.at[0, rows, :], (), lin, base, ROWS, FF)
 
 
 def make_weights(seeds):
@@ -80,7 +87,7 @@
         in_specs=[pl.BlockSpec(memory_space=pltpu.SMEM)],
         out_specs=[spec, spec],
         out_shape=[jax.ShapeDtypeStruct((AHEAD, D, FF), jnp.bfloat16)] * 2,
-        scratch_shapes=[pltpu.VMEM((ROWS, COLS), jnp.int32)],
+        scratch_shapes=[pltpu.VMEM((PIECE, COLS), jnp.int32)],
         compiler_params=pltpu.CompilerParams(vmem_limit_bytes=48 << 20),
         cost_estimate=pl.CostEstimate(
             flops=AHEAD * 2 * D * FF * 600, bytes_accessed=AHEAD * 4 * D * FF, transcendentals=0
@@ -93,7 +100,7 @@
     return (g / (1.0 + jnp.exp(-g)) * (up_part * SCALE_IN) * share).astype(jnp.bfloat16)
 
 
-def up_kernel(seeds, x, share, gate_w, up_w, act, lin, acc):
+def up_kernel(seeds, x, share, gate_w, up_w, act, lin, made, acc):
     expert = pl.program_id(0)
     tile = pl.program_id(1)
 
@@ -104,14 +111,31 @@
     acc[...] = jnp.zeros_like(acc)
     seed = seeds[expert]
 
-    @pl.loop(0, D // ROWS, unroll=2)
-    def _(step):
+    def make(step, slot):
+        for which, salt in enumerate((salt_gate, salt_up)):
+            base = offset(seed, salt, step * ROWS, tile * COLS, FF)
+            hash_rows(made, (slot, which), lin, base, ROWS, FF)
+
+    def use(step, slot):
         rows = pl.ds(pl.multiple_of(step * ROWS, ROWS), ROWS)
         hashed_x, ready_x = x[0, 0, :, rows], x[1, 0, :, rows]
-        for which, (salt, ready) in enumerate(((salt_gate, gate_w), (salt_up, up_w))):
-            w = centred(lin[...] + offset(seed, salt, step * ROWS, tile * COLS, FF))
+        for which, ready in enumerate((gate_w, up_w)):
             acc[2 + which] += jnp.dot(ready_x, ready[0, rows, :], preferred_element_type=jnp.float32)
-            acc[which] += jnp.dot(hashed_x, w, preferred_element_type=jnp.float32)
+            acc[which] += jnp.dot(hashed_x, made[slot, which], preferred_element_type=jnp.float32)
+
+    steps = D // ROWS
+    make(0, 0)
+
+    @pl.loop(0, steps // 2 - 1)
+    def _(pair):
+        make(2 * pair + 1, 1)
+        use(2 * pair, 0)
+        make(2 * pair + 2, 0)
+        use(2 * pair + 1, 1)
+
+    make(steps - 1, 1)
+    use(steps - 2, 0)
+    use(steps - 1, 1)
 
     act[0, 0] = activation(acc[0], acc[1], share[0, 0])
     act[1, 0] = activation(acc[2], acc[3], share[1, 0])
@@ -136,7 +160,8 @@
         out_specs=pl.BlockSpec((2, 1, slots, COLS), lambda e, t: (0, e, 0, t)),
         out_shape=jax.ShapeDtypeStruct((2, half, slots, FF), jnp.bfloat16),
         scratch_shapes=[
-            pltpu.VMEM((ROWS, COLS), jnp.int32),
+            pltpu.VMEM((PIECE, COLS), jnp.int32),
+            pltpu.VMEM((2, 2, ROWS, COLS), jnp.bfloat16),
             pltpu.VMEM((4, slots, COLS), jnp.float32),
         ],
         compiler_params=pltpu.CompilerParams(vmem_limit_bytes=48 << 20),
@@ -146,13 +171,18 @@
     )(seeds, x, share, gate_w, up_w).reshape(experts, slots, FF)
 
 
-def down_kernel(devices, local_count, seeds, act, place, out, lin, y, sent, arrived, send_sem, recv_sem):
-    tile = pl.program_id(0)
-    tiles = pl.num_programs(0)
+def down_kernel(
+    devices, local_count, seeds, act, place, out, lin, made, y, sent, arrived, send_sem, recv_sem
+):
+    step_now = pl.program_id(0)
+    tiles = pl.num_programs(0) - 1
     experts, slots, _ = act.shape
     tok_dev, width = out.shape
     me = lax.axis_index("node") * local_count + lax.axis_index("local")
-    slot = lax.rem(tile, 2)
+    halves = DOWN_COLS // COLS
+    units = experts * halves
+    done = step_now - 1
+    slot = lax.rem(step_now, 2)
 
     def peer(step):
         return lax.rem(me + step, devices)
@@ -162,28 +192,20 @@
 
     barrier = pltpu.get_barrier_semaphore()
 
-    @pl.when(tile == 0)
-    def _():
-        @pl.loop(1, devices)
-        def _(step):
-            pl.semaphore_signal(
-                barrier, inc=1, device_id=device(peer(step)), device_id_type=pl.DeviceIdType.MESH
-            )
-
-        fill_index(lin, D)
-
-    for expert in range(experts):
-        total = jnp.zeros((slots, DOWN_COLS), jnp.float32)
-        for step in range(FF // DOWN_ROWS):
-            w = centred(
-                lin[...] + offset(seeds[expert], salt_down, step * DOWN_ROWS, tile * DOWN_COLS, D)
-            )
-            total += jnp.dot(
-                act[expert, :, step * DOWN_ROWS : (step + 1) * DOWN_ROWS],
-                w,
-                preferred_element_type=jnp.float32,
-            )
-        y[expert * slots : (expert + 1) * slots, :] = (total * SCALE_OUT).astype(jnp.bfloat16)
+    def make(tile, unit):
+        expert, half = unit // halves, unit % halves
+        base = offset(seeds[expert], salt_down, 0, tile * DOWN_COLS + half * COLS, D)
+        hash_rows(made, (unit % 2,), lin, base, FF, D)
+
+    def use(unit):
+        expert, half = unit // halves, unit % halves
+        part = jnp.dot(act[expert], made[unit % 2], preferred_element_type=jnp.float32)
+        y[expert * slots : (expert + 1) * slots, half * COLS : (half + 1) * COLS] = (
+            part * SCALE_OUT
+        ).astype(jnp.bfloat16)
+
+    def combine():
+        sent[slot] = jnp.dot(place[...], y[...], preferred_element_type=jnp.float32).astype(jnp.bfloat16)
 
     def copy(step, where, column):
         to = peer(step)
@@ -196,32 +218,60 @@
             device_id_type=pl.DeviceIdType.MESH,
         )
 
-    @pl.when(tile == 0)
-    def _():
-        pl.semaphore_wait(barrier, devices - 1)
-
-    @pl.when(tile >= 2)
+    @pl.when(step_now == 0)
     def _():
         @pl.loop(1, devices)
         def _(step):
-            copy(step, slot, tile - 2).wait_send()
-
-    sent[slot] = jnp.dot(place[...], y[...], preferred_element_type=jnp.float32).astype(jnp.bfloat16)
-
-    @pl.loop(1, devices)
-    def _(step):
-        copy(step, slot, tile).start()
-
-    own = pl.ds(pl.multiple_of(me * tok_dev, tok_dev), tok_dev)
-    columns = pl.ds(pl.multiple_of(tile * DOWN_COLS, DOWN_COLS), DOWN_COLS)
-    arrived[me, :, columns] = sent[slot, own, :]
-
-    @pl.when(tile == tiles - 1)
+            pl.semaphore_signal(
+                barrier, inc=1, device_id=device(peer(step)), device_id_type=pl.DeviceIdType.MESH
+            )
+
+        fill_index(lin, D)
+        y[...] = jnp.zeros_like(y)
+        make(0, 0)
+
+    @pl.when(step_now == 1)
+    def _():
+        pl.semaphore_wait(barrier, devices - 1)
+
+    @pl.when(step_now >= 3)
     def _():
         @pl.loop(1, devices)
         def _(step):
-            copy(step, 1 - slot, tile - 1).wait_send()
-            copy(step, slot, tile).wait_send()
+            copy(step, slot, done - 2).wait_send()
+
+    @pl.when(step_now < tiles)
+    def _():
+        combine()
+        make(step_now, 1)
+        use(0)
+
+    @pl.when(step_now == tiles)
+    def _():
+        combine()
+
+    @pl.when(step_now >= 1)
+    def _():
+        @pl.loop(1, devices)
+        def _(step):
+            copy(step, slot, done).start()
+
+        own = pl.ds(pl.multiple_of(me * tok_dev, tok_dev), tok_dev)
+        columns = pl.ds(pl.multiple_of(done * DOWN_COLS, DOWN_COLS), DOWN_COLS)
+        arrived[me, :, columns] = sent[slot, own, :]
+
+    @pl.when(step_now < tiles)
+    def _():
+        for unit in range(1, units):
+            make(step_now + (unit + 1) // units, (unit + 1) % units)
+            use(unit)
+
+    @pl.when(step_now == tiles)
+    def _():
+        @pl.loop(1, devices)
+        def _(step):
+            copy(step, 1 - slot, done - 1).wait_send()
+            copy(step, slot, done).wait_send()
             source = peer(step)
             pltpu.make_async_remote_copy(
                 src_ref=arrived.at[source],
@@ -248,7 +298,7 @@
     tokens = place.shape[0]
     return pl.pallas_call(
         functools.partial(down_kernel, devices, local_count),
-        grid=(width // DOWN_COLS,),
+        grid=(width // DOWN_COLS + 1,),
         in_specs=[
             pl.BlockSpec(memory_space=pltpu.SMEM),
             pl.BlockSpec(act.shape, lambda t: (0, 0, 0)),
@@ -257,7 +307,8 @@
         out_specs=pl.BlockSpec((tok_dev, width), lambda t: (0, 0)),
         out_shape=jax.ShapeDtypeStruct((tok_dev, width), jnp.bfloat16),
         scratch_shapes=[
-            pltpu.VMEM((DOWN_ROWS, DOWN_COLS), jnp.int32),
+            pltpu.VMEM((PIECE, COLS), jnp.int32),
+            pltpu.VMEM((2, FF, COLS), jnp.bfloat16),
             pltpu.VMEM((experts * slots, DOWN_COLS), jnp.bfloat16),
             pltpu.VMEM((2, tokens, DOWN_COLS), jnp.bfloat16),
             pltpu.VMEM((devices, tok_dev, width), jnp.bfloat16),

time: 252 us -> 247 us (0.980)
  Pallas kernels: 216 us -> 210 us
    pallas_call x1, Pallas kernels: 56.1 us -> 52.5 us  [make_weights(): pl.pallas_call(make_kernel, grid=(AHEAD, FF // COLS), in_specs=[pl.BlockS...]
    pallas_call x1, Pallas kernels: 68.4 us -> 65.3 us  [run_up(): pl.pallas_call(up_kernel, grid=(half, FF // COLS), in_specs=[pl.BlockSpec...]
  transfers between devices with their start and end apart: 1 -> 1, of which waited for: 0 -> 1; matrix products, arithmetic and copies ran while one was open for 0% -> 0% of each run, Pallas kernels for 22% -> 21%
where the time goes in v3:
time: 247 us; the launch traced here: 246 us
  Pallas kernels  210 us (85%)
  between operations  13.5 us (5%)
  matrix products  9.54 us (4%)
  local copies, waits for them, and re-layouts  6.71 us (3%)
  other arithmetic  5.87 us (2%)
    pallas_call x1, Pallas kernels, run_down(): pl.pallas_call(functools.partial(down_kernel, devices, local_count), grid...  92.6 us
    pallas_call x1, Pallas kernels, run_up(): pl.pallas_call(up_kernel, grid=(half, FF // COLS), in_specs=[pl.BlockSpec...  65.3 us
    pallas_call x1, Pallas kernels, make_weights(): pl.pallas_call(make_kernel, grid=(AHEAD, FF // COLS), in_specs=[pl.BlockS...  52.5 us
    dot_general x1, matrix products, on_device(): jnp.dot(pick.reshape(EXP_DEV * slots, -1), every, preferred_element_type=...  9.34 us
  transfers between devices with their start and end apart: 1, of which 1 were waited for; matrix products, arithmetic and copies ran while one was open for 0% of the time, Pallas kernels for 21%

profile of v3, /device:TPU:0, one launch (start us, length us, event | category | flops | bytes accessed | tf_op | source)
XLA Modules:
  0.0 246.2 jit_solution(3139029001026382537)
XLA Ops:
  6.5 0.0 all-gather.2.cloned.1.call-start
  6.5 0.7 convert.11
  7.2 0.7 convert.9
  7.9 0.7 convert.10
  8.6 0.1 copy.20
  8.7 2.2 fusion.3
  10.9 0.0 all-gather.2.cloned.1.call-update
  11.0 0.0 copy-start.1
  11.0 0.6 copy-done.1
  11.6 52.5 %shard_map.55 = (bf16[2,7168,1024]{2,1,0:T(8,128)(2,1)}, bf16[2,7168,1024]{2,1,0:T(8,128)(2,1)}) custom-call(s32[4]{0:T(128)S(1)} %copy-done.1), custom_call_target="tpu_custom_call" | custom-call | flops 17616076800 | bytes 58720256 | tf_op jit(solution)/shard_map/pallas_call | solution.py:84
  64.1 0.2 all-gather.2.cloned.1.call-done
  64.3 0.9 slice.16
  65.2 0.1 copy.24
  65.4 0.1 fusion.4
  65.5 0.1 select_reduce_fusion.1
  65.6 0.1 reshape.66
  65.7 0.2 fusion.1
  65.9 0.1 convert_element_type.35
  66.0 0.1 copy.23
  66.2 0.2 select_reduce_fusion
  66.4 0.2 copy.22.share
  66.5 1.3 eq.84
  67.8 1.1 fusion.2
  69.0 0.0 copy-start.2
  69.0 9.3 %convolution_convert_fusion = bf16[512,7296]{1,0:T(8,128)(2,1)} fusion(pred[512,512]{1,0:T(32,128)(4,1)S(1)} %get-tuple-element.12, bf16[512,7296]{1,0:T(8,128)(2,1)} %all-gather.2.cloned.1.call-done), kind=kOutput, calls=%fused_computation | convolution fusion | flops 3828940800 | bytes 15204352 | tf_op jit(solution)/shard_map/dot_general | solution.py:377
  78.3 0.0 copy-done.2
  78.3 65.3 %shard_map.56 = bf16[2,2,128,1024]{3,2,1,0:T(8,128)(2,1)S(1)} custom-call(s32[4]{0:T(128)S(1)} %copy-done.2, bf16[2,2,128,7296]{3,2,1,0:T(8,128)(2,1)} %bitcast.27, f32[2,2,128,1]{3,2,1,0:T(8,128)S(1)} %copy.22.share, bf16[2,7168,1024]{2,1,0:T(8,128)(2,1)} %get-tuple-element.7.gate_w, bf16[2,7168,1024]{2,1,0:T(8,128)(2,1)} %get-tuple-element.8.up_w), custom_call_target="tpu_custom_call" | custom-call | flops 17616076800 | bytes 7471104 | tf_op jit(solution)/shard_map/pallas_call | solution.py:150
  143.6 0.0 copy-start
  143.6 1.0 copy-done
  144.6 92.6 %shard_map.57 = bf16[64,7168]{1,0:T(8,128)(2,1)} custom-call(s32[4]{0:T(128)} %seeds.5, bf16[4,128,1024]{2,1,0:T(8,128)(2,1)} %bitcast.26, bf16[512,512]{1,0:T(8,128)(2,1)} %get-tuple-element.11.place), custom_call_target="tpu_custom_call" | custom-call | flops 35232153600 | bytes 7340032 | tf_op jit(solution)/shard_map/pallas_call | solution.py:299
  237.2 2.2 copy.32
  (12 shorter events, 0.1 us)
Async XLA Ops:
  6.5 57.8 %all-gather.2.cloned.1.call-start = ((), (), s32[]{:S(2)}) async-start(), calls=%async_computation | async-start | bytes 8404992 | tf_op jit(solution)/shard_map/all_gather | solution.py:366
  11.0 0.7 copy-start.1
  69.0 9.3 %copy-start.2 = (s32[4]{0:T(128)S(1)}, s32[4]{0:T(128)}, u32[]{:S(2)}) copy-start(s32[4]{0:T(128)} %seeds.5) | copy-start | bytes 52
  143.6 1.0 copy-start
Sparse Core Ops, SparseCore 0:
  11.0 53.1 all-gather.1

commit v4 on v3

--- a/solution.py
+++ b/solution.py
@@ -171,24 +171,43 @@
     )(seeds, x, share, gate_w, up_w).reshape(experts, slots, FF)
 
 
+def pairs_along_node(nodes, locals_):
+    return locals_ < nodes
+
+
 def down_kernel(
-    devices, local_count, seeds, act, place, out, lin, made, y, sent, arrived, send_sem, recv_sem
+    nodes, locals_, seeds, act, place, out,
+    lin, made, y, sent, paired, pushed, arrived,
+    pair_send, pair_recv, push_send, push_recv,
 ):
     step_now = pl.program_id(0)
-    tiles = pl.num_programs(0) - 1
+    tiles = pl.num_programs(0) - 2
     experts, slots, _ = act.shape
     tok_dev, width = out.shape
-    me = lax.axis_index("node") * local_count + lax.axis_index("local")
+    node, local = lax.axis_index("node"), lax.axis_index("local")
+    half_devices = nodes * locals_ // 2
+    by_node = pairs_along_node(nodes, locals_)
+    side = lax.rem(node, 2) if by_node else lax.rem(local, 2)
+    me = node // 2 * locals_ + local if by_node else node * (locals_ // 2) + local // 2
     halves = DOWN_COLS // COLS
     units = experts * halves
     done = step_now - 1
+    onward = step_now - 2
     slot = lax.rem(step_now, 2)
 
+    def device(index):
+        if by_node:
+            return {"node": index // locals_ * 2 + side, "local": lax.rem(index, locals_)}
+        per_node = locals_ // 2
+        return {"node": index // per_node, "local": lax.rem(index, per_node) * 2 + side}
+
     def peer(step):
-        return lax.rem(me + step, devices)
-
-    def device(index):
-        return {"node": index // local_count, "local": lax.rem(index, local_count)}
+        return lax.rem(me + step, half_devices)
+
+    if by_node:
+        sibling = {"node": node + 1 - 2 * side, "local": local}
+    else:
+        sibling = {"node": node, "local": local + 1 - 2 * side}
 
     barrier = pltpu.get_barrier_semaphore()
 
@@ -207,24 +226,44 @@
     def combine():
         sent[slot] = jnp.dot(place[...], y[...], preferred_element_type=jnp.float32).astype(jnp.bfloat16)
 
-    def copy(step, where, column):
+    def block(index):
+        return pl.ds(pl.multiple_of(index * tok_dev, tok_dev), tok_dev)
+
+    def columns(tile):
+        return pl.ds(pl.multiple_of(tile * DOWN_COLS, DOWN_COLS), DOWN_COLS)
+
+    def pair_copy(where, tile):
+        rows = half_devices * tok_dev
+        return pltpu.make_async_remote_copy(
+            src_ref=sent.at[where, pl.ds(pl.multiple_of((1 - side) * rows, rows), rows), :],
+            dst_ref=paired.at[:, columns(tile)],
+            send_sem=pair_send.at[where],
+            recv_sem=pair_recv.at[tile],
+            device_id=sibling,
+            device_id_type=pl.DeviceIdType.MESH,
+        )
+
+    def push(step, where, tile):
         to = peer(step)
         return pltpu.make_async_remote_copy(
-            src_ref=sent.at[where, pl.ds(pl.multiple_of(to * tok_dev, tok_dev), tok_dev), :],
-            dst_ref=arrived.at[me, :, pl.ds(pl.multiple_of(column * DOWN_COLS, DOWN_COLS), DOWN_COLS)],
-            send_sem=send_sem.at[where, to],
-            recv_sem=recv_sem.at[me],
+            src_ref=pushed.at[where, block(to), :],
+            dst_ref=arrived.at[me, :, columns(tile)],
+            send_sem=push_send.at[where, to],
+            recv_sem=push_recv.at[me],
             device_id=device(to),
             device_id_type=pl.DeviceIdType.MESH,
         )
 
+    def greet(other):
+        pl.semaphore_signal(barrier, inc=1, device_id=other, device_id_type=pl.DeviceIdType.MESH)
+
     @pl.when(step_now == 0)
     def _():
-        @pl.loop(1, devices)
+        greet(sibling)
+
+        @pl.loop(1, half_devices)
         def _(step):
-            pl.semaphore_signal(
-                barrier, inc=1, device_id=device(peer(step)), device_id_type=pl.DeviceIdType.MESH
-            )
+            greet(device(peer(step)))
 
         fill_index(lin, D)
         y[...] = jnp.zeros_like(y)
@@ -232,13 +271,33 @@
 
     @pl.when(step_now == 1)
     def _():
-        pl.semaphore_wait(barrier, devices - 1)
-
-    @pl.when(step_now >= 3)
-    def _():
-        @pl.loop(1, devices)
+        pl.semaphore_wait(barrier, half_devices)
+
+    @pl.when(step_now >= 4)
+    def _():
+        @pl.loop(1, half_devices)
         def _(step):
-            copy(step, slot, done - 2).wait_send()
+            push(step, slot, onward - 2).wait_send()
+
+    @pl.when(step_now >= 2)
+    def _():
+        pair_copy(1 - slot, onward).wait_recv()
+
+        @pl.loop(0, half_devices)
+        def _(index):
+            mine = sent[1 - slot, block(side * half_devices + index), :].astype(jnp.float32)
+            theirs = paired[block(index), columns(onward)].astype(jnp.float32)
+            pushed[slot, block(index), :] = (mine + theirs).astype(jnp.bfloat16)
+
+        @pl.loop(1, half_devices)
+        def _(step):
+            push(step, slot, onward).start()
+
+        arrived[me, :, columns(onward)] = pushed[slot, block(me), :]
+
+    @pl.when((step_now >= 3) & (step_now <= tiles))
+    def _():
+        pair_copy(slot, done - 2).wait_send()
 
     @pl.when(step_now < tiles)
     def _():
@@ -250,15 +309,9 @@
     def _():
         combine()
 
-    @pl.when(step_now >= 1)
-    def _():
-        @pl.loop(1, devices)
-        def _(step):
-            copy(step, slot, done).start()
-
-        own = pl.ds(pl.multiple_of(me * tok_dev, tok_dev), tok_dev)
-        columns = pl.ds(pl.multiple_of(done * DOWN_COLS, DOWN_COLS), DOWN_COLS)
-        arrived[me, :, columns] = sent[slot, own, :]
+    @pl.when((step_now >= 1) & (step_now <= tiles))
+    def _():
+        pair_copy(slot, done).start()
 
     @pl.when(step_now < tiles)
     def _():
@@ -266,39 +319,42 @@
             make(step_now + (unit + 1) // units, (unit + 1) % units)
             use(unit)
 
-    @pl.when(step_now == tiles)
-    def _():
-        @pl.loop(1, devices)
+    @pl.when(step_now == tiles + 1)
+    def _():
+        pair_copy(slot, tiles - 2).wait_send()
+        pair_copy(1 - slot, tiles - 1).wait_send()
+
+        @pl.loop(1, half_devices)
         def _(step):
-            copy(step, 1 - slot, done - 1).wait_send()
-            copy(step, slot, done).wait_send()
+            push(step, 1 - slot, onward - 1).wait_send()
+            push(step, slot, onward).wait_send()
             source = peer(step)
             pltpu.make_async_remote_copy(
                 src_ref=arrived.at[source],
                 dst_ref=arrived.at[source],
-                send_sem=send_sem.at[0, source],
-                recv_sem=recv_sem.at[source],
+                send_sem=push_send.at[0, source],
+                recv_sem=push_recv.at[source],
                 device_id=device(source),
                 device_id_type=pl.DeviceIdType.MESH,
             ).wait_recv()
 
         @pl.loop(0, width // DOWN_COLS)
         def _(part):
-            span = pl.ds(pl.multiple_of(part * DOWN_COLS, DOWN_COLS), DOWN_COLS)
-
             def add(source, total):
-                return total + arrived[source, :, span].astype(jnp.float32)
-
-            total = lax.fori_loop(0, devices, add, jnp.zeros((tok_dev, DOWN_COLS), jnp.float32))
-            out[:, span] = total.astype(jnp.bfloat16)
-
-
-def run_down(seeds, act, place, tok_dev, width, devices, local_count):
+                return total + arrived[source, :, columns(part)].astype(jnp.float32)
+
+            total = lax.fori_loop(0, half_devices, add, jnp.zeros((tok_dev, DOWN_COLS), jnp.float32))
+            out[:, columns(part)] = total.astype(jnp.bfloat16)
+
+
+def run_down(seeds, act, place, tok_dev, width, nodes, locals_):
     experts, slots, _ = act.shape
+    half_devices = nodes * locals_ // 2
+    tiles = width // DOWN_COLS
     tokens = place.shape[0]
     return pl.pallas_call(
-        functools.partial(down_kernel, devices, local_count),
-        grid=(width // DOWN_COLS + 1,),
+        functools.partial(down_kernel, nodes, locals_),
+        grid=(tiles + 2,),
         in_specs=[
             pl.BlockSpec(memory_space=pltpu.SMEM),
             pl.BlockSpec(act.shape, lambda t: (0, 0, 0)),
@@ -311,9 +367,13 @@
             pltpu.VMEM((2, FF, COLS), jnp.bfloat16),
             pltpu.VMEM((experts * slots, DOWN_COLS), jnp.bfloat16),
             pltpu.VMEM((2, tokens, DOWN_COLS), jnp.bfloat16),
-            pltpu.VMEM((devices, tok_dev, width), jnp.bfloat16),
-            pltpu.SemaphoreType.DMA((2, devices)),
-            pltpu.SemaphoreType.DMA((devices,)),
+            pltpu.VMEM((tokens // 2, width), jnp.bfloat16),
+            pltpu.VMEM((2, tokens // 2, DOWN_COLS), jnp.bfloat16),
+            pltpu.VMEM((half_devices, tok_dev, width), jnp.bfloat16),
+            pltpu.SemaphoreType.DMA((2,)),
+            pltpu.SemaphoreType.DMA((tiles,)),
+            pltpu.SemaphoreType.DMA((2, half_devices)),
+            pltpu.SemaphoreType.DMA((half_devices,)),
         ],
         compiler_params=pltpu.CompilerParams(
             vmem_limit_bytes=56 << 20, collective_id=0, has_side_effects=True
@@ -378,7 +438,13 @@
         pick.reshape(EXP_DEV * slots, -1), every, preferred_element_type=jnp.float32
     ).astype(jnp.bfloat16).reshape(EXP_DEV, slots, -1)
     act = run_up(expert_seeds, x, share, gate_w, up_w)
-    return run_down(expert_seeds, act, place, tok_dev, width, devices_all, local_count)
+    nodes = devices_all // local_count
+    if pairs_along_node(nodes, local_count):
+        place = place.reshape(nodes // 2, 2, local_count, tok_dev, -1).transpose(1, 0, 2, 3, 4)
+    else:
+        place = place.reshape(nodes, local_count // 2, 2, tok_dev, -1).transpose(2, 0, 1, 3, 4)
+    place = place.reshape(devices_all * tok_dev, -1)
+    return run_down(expert_seeds, act, place, tok_dev, width, nodes, local_count)
 
 
 def solution(mesh):

time: 247 us -> 228 us (0.923)
  Pallas kernels: 210 us -> 192 us
    pallas_call x1, Pallas kernels: 92.6 us -> 73.7 us  [run_down(): pl.pallas_call(functools.partial(down_kernel, nodes, locals_), grid=(tile...]
  transfers between devices with their start and end apart: 1 -> 1, of which waited for: 1 -> 1; matrix products, arithmetic and copies ran while one was open for 0% -> 0% of each run, Pallas kernels for 21% -> 23%
where the time goes in v4:
time: 228 us
  Pallas kernels  192 us (84%)
  between operations  13.6 us (6%)
  matrix products  9.52 us (4%)
  local copies, waits for them, and re-layouts  7.96 us (3%)
  other arithmetic  5.09 us (2%)
    pallas_call x1, Pallas kernels, run_down(): pl.pallas_call(functools.partial(down_kernel, nodes, locals_), grid=(tile...  73.7 us
    pallas_call x1, Pallas kernels, run_up(): pl.pallas_call(up_kernel, grid=(half, FF // COLS), in_specs=[pl.BlockSpec...  65.3 us
    pallas_call x1, Pallas kernels, make_weights(): pl.pallas_call(make_kernel, grid=(AHEAD, FF // COLS), in_specs=[pl.BlockS...  52.5 us
    dot_general x1, matrix products, on_device(): jnp.dot(pick.reshape(EXP_DEV * slots, -1), every, preferred_element_type=...  9.33 us
  transfers between devices with their start and end apart: 1, of which 1 were waited for; matrix products, arithmetic and copies ran while one was open for 0% of the time, Pallas kernels for 23%

profile of v4, /device:TPU:0, one launch (start us, length us, event | category | flops | bytes accessed | tf_op | source)
XLA Modules:
  0.0 227.8 jit_solution(11006410374772054211)
XLA Ops:
  6.5 0.0 all-gather.2.cloned.1.call-start
  6.5 0.7 convert.11
  7.2 0.7 convert.12
  7.9 0.7 convert.13
  8.6 0.1 copy.23
  8.7 2.2 fusion.2
  10.9 0.0 all-gather.2.cloned.1.call-update
  11.0 0.0 copy-start.1
  11.0 0.6 copy-done.1
  11.6 52.5 %shard_map.55 = (bf16[2,7168,1024]{2,1,0:T(8,128)(2,1)}, bf16[2,7168,1024]{2,1,0:T(8,128)(2,1)}) custom-call(s32[4]{0:T(128)S(1)} %copy-done.1), custom_call_target="tpu_custom_call" | custom-call | flops 17616076800 | bytes 58720256 | tf_op jit(solution)/shard_map/pallas_call | solution.py:84
  64.1 0.2 all-gather.2.cloned.1.call-done
  64.3 0.9 slice.16
  65.2 0.1 copy.28
  65.4 0.1 fusion.4
  65.5 0.1 reshape.70
  65.6 0.2 fusion.1
  65.8 0.1 convert_element_type.33
  65.9 0.1 select_reduce_fusion.1
  66.0 0.1 copy.26
  66.2 0.2 select_reduce_fusion
  66.4 0.2 copy.25.share
  66.5 0.2 bitcast_compare_fusion
  66.7 1.3 eq.84
  68.1 0.4 eq.85
  68.5 0.1 fusion.3
  68.6 0.8 copy.27
  69.5 0.0 copy-start.2
  69.5 9.3 %convolution_convert_fusion = bf16[512,7296]{1,0:T(8,128)(2,1)} fusion(pred[512,512]{1,0:T(32,128)(4,1)S(1)} %bitcast_compare_fusion, bf16[512,7296]{1,0:T(8,128)(2,1)} %all-gather.2.cloned.1.call-done), kind=kOutput, calls=%fused_computation | convolution fusion | flops 3828940800 | bytes 15204352 | tf_op jit(solution)/shard_map/dot_general | solution.py:437
  78.8 0.0 copy-done.2
  78.8 65.3 %shard_map.56 = bf16[2,2,128,1024]{3,2,1,0:T(8,128)(2,1)S(1)} custom-call(s32[4]{0:T(128)S(1)} %copy-done.2, bf16[2,2,128,7296]{3,2,1,0:T(8,128)(2,1)} %bitcast.25, f32[2,2,128,1]{3,2,1,0:T(8,128)S(1)} %copy.25.share, bf16[2,7168,1024]{2,1,0:T(8,128)(2,1)} %get-tuple-element.7.gate_w, bf16[2,7168,1024]{2,1,0:T(8,128)(2,1)} %get-tuple-element.8.up_w), custom_call_target="tpu_custom_call" | custom-call | flops 17616076800 | bytes 7471104 | tf_op jit(solution)/shard_map/pallas_call | solution.py:150
  144.1 0.0 copy-start
  144.1 1.0 copy-done
  145.1 73.7 %shard_map.57 = bf16[64,7168]{1,0:T(8,128)(2,1)} custom-call(s32[4]{0:T(128)} %seeds.5, bf16[4,128,1024]{2,1,0:T(8,128)(2,1)} %bitcast.24, bf16[512,512]{1,0:T(8,128)(2,1)} %bitcast.26), custom_call_target="tpu_custom_call" | custom-call | flops 35232153600 | bytes 7340032 | tf_op jit(solution)/shard_map/pallas_call | solution.py:355
  218.8 2.2 copy.32
  (12 shorter events, 0.1 us)
Async XLA Ops:
  6.5 57.8 %all-gather.2.cloned.1.call-start = ((), (), s32[]{:S(2)}) async-start(), calls=%async_computation | async-start | bytes 8404992 | tf_op jit(solution)/shard_map/all_gather | solution.py:426
  11.0 0.7 copy-start.1
  69.5 9.3 %copy-start.2 = (s32[4]{0:T(128)S(1)}, s32[4]{0:T(128)}, u32[]{:S(2)}) copy-start(s32[4]{0:T(128)} %seeds.5) | copy-start | bytes 52
  144.1 1.0 copy-start
Sparse Core Ops, SparseCore 0:
  11.0 53.1 all-gather.1

commit v5 on v4

--- a/solution.py
+++ b/solution.py
@@ -100,7 +100,7 @@
     return (g / (1.0 + jnp.exp(-g)) * (up_part * SCALE_IN) * share).astype(jnp.bfloat16)
 
 
-def up_kernel(seeds, x, share, gate_w, up_w, act, lin, made, acc):
+def up_kernel(first, seeds, x, share, gate_w, up_w, act, lin, made, acc):
     expert = pl.program_id(0)
     tile = pl.program_id(1)
 
@@ -113,7 +113,7 @@
 
     def make(step, slot):
         for which, salt in enumerate((salt_gate, salt_up)):
-            base = offset(seed, salt, step * ROWS, tile * COLS, FF)
+            base = offset(seed, salt, step * ROWS, (first + tile) * COLS, FF)
             hash_rows(made, (slot, which), lin, base, ROWS, FF)
 
     def use(step, slot):
@@ -141,15 +141,15 @@
     act[1, 0] = activation(acc[2], acc[3], share[1, 0])
 
 
-def run_up(seeds, x, share, gate_w, up_w):
+def run_up(seeds, x, share, gate_w, up_w, first, count):
     experts, slots, _ = x.shape
     half = experts - AHEAD
     x = x.reshape(2, half, slots, -1)
     share = share.reshape(2, half, slots, 1)
-    weights = pl.BlockSpec((1, D, COLS), lambda e, t: (e, 0, t))
+    weights = pl.BlockSpec((1, D, COLS), lambda e, t: (e, 0, first + t))
     return pl.pallas_call(
-        up_kernel,
-        grid=(half, FF // COLS),
+        functools.partial(up_kernel, first),
+        grid=(half, count),
         in_specs=[
             pl.BlockSpec(memory_space=pltpu.SMEM),
             pl.BlockSpec((2, 1, slots, D), lambda e, t: (0, e, 0, 0)),
@@ -158,7 +158,7 @@
             weights,
         ],
         out_specs=pl.BlockSpec((2, 1, slots, COLS), lambda e, t: (0, e, 0, t)),
-        out_shape=jax.ShapeDtypeStruct((2, half, slots, FF), jnp.bfloat16),
+        out_shape=jax.ShapeDtypeStruct((2, half, slots, count * COLS), jnp.bfloat16),
         scratch_shapes=[
             pltpu.VMEM((PIECE, COLS), jnp.int32),
             pltpu.VMEM((2, 2, ROWS, COLS), jnp.bfloat16),
@@ -166,9 +166,9 @@
         ],
         compiler_params=pltpu.CompilerParams(vmem_limit_bytes=48 << 20),
         cost_estimate=pl.CostEstimate(
-            flops=half * 2 * D * FF * 600, bytes_accessed=2 * x.size, transcendentals=0
+            flops=half * 2 * D * count * COLS * 600, bytes_accessed=2 * x.size, transcendentals=0
         ),
-    )(seeds, x, share, gate_w, up_w).reshape(experts, slots, FF)
+    )(seeds, x, share, gate_w, up_w).reshape(experts, slots, count * COLS)
 
 
 def pairs_along_node(nodes, locals_):
@@ -176,14 +176,18 @@
 
 
 def down_kernel(
-    nodes, locals_, seeds, act, place, out,
+    nodes, locals_, seeds, act_main, act_rest, other_main, other_rest, place, out,
     lin, made, y, sent, paired, pushed, arrived,
     pair_send, pair_recv, push_send, push_recv,
 ):
     step_now = pl.program_id(0)
     tiles = pl.num_programs(0) - 2
-    experts, slots, _ = act.shape
+    experts, slots, main = act_main.shape
     tok_dev, width = out.shape
+    part_width = width // 2
+    rep = lax.axis_index("rep")
+    zside = lax.rem(rep, 2)
+    partner = rep + 1 - 2 * zside
     node, local = lax.axis_index("node"), lax.axis_index("local")
     half_devices = nodes * locals_ // 2
     by_node = pairs_along_node(nodes, locals_)
@@ -201,30 +205,57 @@
         per_node = locals_ // 2
         return {"node": index // per_node, "local": lax.rem(index, per_node) * 2 + side}
 
+    def target(which, index):
+        return {"rep": partner if which else rep, **device(index)}
+
     def peer(step):
         return lax.rem(me + step, half_devices)
 
+    def each_target(act_on):
+        @pl.loop(0, half_devices)
+        def _(step):
+            act_on(1, step)
+
+        @pl.loop(1, half_devices)
+        def _(step):
+            act_on(0, step)
+
     if by_node:
-        sibling = {"node": node + 1 - 2 * side, "local": local}
+        sibling = {"rep": rep, "node": node + 1 - 2 * side, "local": local}
     else:
-        sibling = {"node": node, "local": local + 1 - 2 * side}
+        sibling = {"rep": rep, "node": node, "local": local + 1 - 2 * side}
 
     barrier = pltpu.get_barrier_semaphore()
 
     def make(tile, unit):
         expert, half = unit // halves, unit % halves
-        base = offset(seeds[expert], salt_down, 0, tile * DOWN_COLS + half * COLS, D)
+        base = offset(
+            seeds[expert], salt_down, 0, zside * part_width + tile * DOWN_COLS + half * COLS, D
+        )
         hash_rows(made, (unit % 2,), lin, base, FF, D)
 
     def use(unit):
         expert, half = unit // halves, unit % halves
-        part = jnp.dot(act[expert], made[unit % 2], preferred_element_type=jnp.float32)
-        y[expert * slots : (expert + 1) * slots, half * COLS : (half + 1) * COLS] = (
-            part * SCALE_OUT
-        ).astype(jnp.bfloat16)
+        rows_main = jnp.concatenate([act_main[expert], other_main[expert]], axis=0)
+        rows_rest = jnp.concatenate([act_rest[expert], other_rest[expert]], axis=0)
+        part = jnp.dot(rows_main, made[unit % 2, :main], preferred_element_type=jnp.float32)
+        part += jnp.dot(rows_rest, made[unit % 2, main:], preferred_element_type=jnp.float32)
+        part = (part * SCALE_OUT).astype(jnp.bfloat16)
+        for which in range(2):
+            y[
+                which, expert * slots : (expert + 1) * slots, half * COLS : (half + 1) * COLS
+            ] = part[which * slots : (which + 1) * slots]
+
+    rows = half_devices * tok_dev
 
     def combine():
-        sent[slot] = jnp.dot(place[...], y[...], preferred_element_type=jnp.float32).astype(jnp.bfloat16)
+        for which in range(2):
+            for part in range(2):
+                sent[slot, part, which] = jnp.dot(
+                    place[which, part * rows : (part + 1) * rows],
+                    y[which],
+                    preferred_element_type=jnp.float32,
+                ).astype(jnp.bfloat16)
 
     def block(index):
         return pl.ds(pl.multiple_of(index * tok_dev, tok_dev), tok_dev)
@@ -233,24 +264,23 @@
         return pl.ds(pl.multiple_of(tile * DOWN_COLS, DOWN_COLS), DOWN_COLS)
 
     def pair_copy(where, tile):
-        rows = half_devices * tok_dev
         return pltpu.make_async_remote_copy(
-            src_ref=sent.at[where, pl.ds(pl.multiple_of((1 - side) * rows, rows), rows), :],
-            dst_ref=paired.at[:, columns(tile)],
+            src_ref=sent.at[where, 1 - side],
+            dst_ref=paired.at[:, :, columns(tile)],
             send_sem=pair_send.at[where],
             recv_sem=pair_recv.at[tile],
             device_id=sibling,
             device_id_type=pl.DeviceIdType.MESH,
         )
 
-    def push(step, where, tile):
+    def push(which, step, where, tile):
         to = peer(step)
         return pltpu.make_async_remote_copy(
-            src_ref=pushed.at[where, block(to), :],
-            dst_ref=arrived.at[me, :, columns(tile)],
-            send_sem=push_send.at[where, to],
-            recv_sem=push_recv.at[me],
-            device_id=device(to),
+            src_ref=pushed.at[where, which, block(to), :],
+            dst_ref=arrived.at[which, me, :, columns(tile)],
+            send_sem=push_send.at[where, which, to],
+            recv_sem=push_recv.at[which, me],
+            device_id=target(which, to),
             device_id_type=pl.DeviceIdType.MESH,
         )
 
@@ -261,9 +291,7 @@
     def _():
         greet(sibling)
 
-        @pl.loop(1, half_devices)
-        def _(step):
-            greet(device(peer(step)))
+        each_target(lambda which, step: greet(target(which, peer(step))))
 
         fill_index(lin, D)
         y[...] = jnp.zeros_like(y)
@@ -271,13 +299,11 @@
 
     @pl.when(step_now == 1)
     def _():
-        pl.semaphore_wait(barrier, half_devices)
+        pl.semaphore_wait(barrier, 2 * half_devices)
 
     @pl.when(step_now >= 4)
     def _():
-        @pl.loop(1, half_devices)
-        def _(step):
-            push(step, slot, onward - 2).wait_send()
+        each_target(lambda which, step: push(which, step, slot, onward - 2).wait_send())
 
     @pl.when(step_now >= 2)
     def _():
@@ -285,15 +311,13 @@
 
         @pl.loop(0, half_devices)
         def _(index):
-            mine = sent[1 - slot, block(side * half_devices + index), :].astype(jnp.float32)
-            theirs = paired[block(index), columns(onward)].astype(jnp.float32)
-            pushed[slot, block(index), :] = (mine + theirs).astype(jnp.bfloat16)
-
-        @pl.loop(1, half_devices)
-        def _(step):
-            push(step, slot, onward).start()
-
-        arrived[me, :, columns(onward)] = pushed[slot, block(me), :]
+            for which in range(2):
+                mine = sent[1 - slot, side, which, block(index), :].astype(jnp.float32)
+                theirs = paired[which, block(index), columns(onward)].astype(jnp.float32)
+                pushed[slot, which, block(index), :] = (mine + theirs).astype(jnp.bfloat16)
+
+        each_target(lambda which, step: push(which, step, slot, onward).start())
+        arrived[0, me, :, columns(onward)] = pushed[slot, 0, block(me), :]
 
     @pl.when((step_now >= 3) & (step_now <= tiles))
     def _():
@@ -324,64 +348,71 @@
         pair_copy(slot, tiles - 2).wait_send()
         pair_copy(1 - slot, tiles - 1).wait_send()
 
-        @pl.loop(1, half_devices)
-        def _(step):
-            push(step, 1 - slot, onward - 1).wait_send()
-            push(step, slot, onward).wait_send()
+        def finish(which, step):
+            push(which, step, 1 - slot, onward - 1).wait_send()
+            push(which, step, slot, onward).wait_send()
             source = peer(step)
             pltpu.make_async_remote_copy(
-                src_ref=arrived.at[source],
-                dst_ref=arrived.at[source],
-                send_sem=push_send.at[0, source],
-                recv_sem=push_recv.at[source],
-                device_id=device(source),
+                src_ref=arrived.at[which, source],
+                dst_ref=arrived.at[which, source],
+                send_sem=push_send.at[0, which, source],
+                recv_sem=push_recv.at[which, source],
+                device_id=target(which, source),
                 device_id_type=pl.DeviceIdType.MESH,
             ).wait_recv()
 
-        @pl.loop(0, width // DOWN_COLS)
-        def _(part):
-            def add(source, total):
-                return total + arrived[source, :, columns(part)].astype(jnp.float32)
-
-            total = lax.fori_loop(0, half_devices, add, jnp.zeros((tok_dev, DOWN_COLS), jnp.float32))
-            out[:, columns(part)] = total.astype(jnp.bfloat16)
-
-
-def run_down(seeds, act, place, tok_dev, width, nodes, locals_):
-    experts, slots, _ = act.shape
+        each_target(finish)
+
+        for which in range(2):
+            start = (zside if which == 0 else 1 - zside) * part_width
+
+            @pl.loop(0, part_width // DOWN_COLS)
+            def _(part):
+                def add(source, total):
+                    return total + arrived[which, source, :, columns(part)].astype(jnp.float32)
+
+                total = lax.fori_loop(
+                    0, half_devices, add, jnp.zeros((tok_dev, DOWN_COLS), jnp.float32)
+                )
+                span = pl.ds(pl.multiple_of(start + part * DOWN_COLS, DOWN_COLS), DOWN_COLS)
+                out[:, span] = total.astype(jnp.bfloat16)
+
+
+def run_down(seeds, acts, place, tok_dev, width, nodes, locals_):
+    experts, slots, _ = acts[0].shape
     half_devices = nodes * locals_ // 2
-    tiles = width // DOWN_COLS
-    tokens = place.shape[0]
+    tiles = width // 2 // DOWN_COLS
+    tokens = place.shape[1]
     return pl.pallas_call(
         functools.partial(down_kernel, nodes, locals_),
         grid=(tiles + 2,),
         in_specs=[
             pl.BlockSpec(memory_space=pltpu.SMEM),
-            pl.BlockSpec(act.shape, lambda t: (0, 0, 0)),
-            pl.BlockSpec(place.shape, lambda t: (0, 0)),
+            *[pl.BlockSpec(act.shape, lambda t: (0, 0, 0)) for act in acts],
+            pl.BlockSpec(place.shape, lambda t: (0, 0, 0)),
         ],
         out_specs=pl.BlockSpec((tok_dev, width), lambda t: (0, 0)),
         out_shape=jax.ShapeDtypeStruct((tok_dev, width), jnp.bfloat16),
         scratch_shapes=[
             pltpu.VMEM((PIECE, COLS), jnp.int32),
             pltpu.VMEM((2, FF, COLS), jnp.bfloat16),
-            pltpu.VMEM((experts * slots, DOWN_COLS), jnp.bfloat16),
-            pltpu.VMEM((2, tokens, DOWN_COLS), jnp.bfloat16),
-            pltpu.VMEM((tokens // 2, width), jnp.bfloat16),
-            pltpu.VMEM((2, tokens // 2, DOWN_COLS), jnp.bfloat16),
-            pltpu.VMEM((half_devices, tok_dev, width), jnp.bfloat16),
+            pltpu.VMEM((2, experts * slots, DOWN_COLS), jnp.bfloat16),
+            pltpu.VMEM((2, 2, 2, tokens // 2, DOWN_COLS), jnp.bfloat16),
+            pltpu.VMEM((2, tokens // 2, width // 2), jnp.bfloat16),
+            pltpu.VMEM((2, 2, tokens // 2, DOWN_COLS), jnp.bfloat16),
+            pltpu.VMEM((2, half_devices, tok_dev, width // 2), jnp.bfloat16),
             pltpu.SemaphoreType.DMA((2,)),
             pltpu.SemaphoreType.DMA((tiles,)),
+            pltpu.SemaphoreType.DMA((2, 2, half_devices)),
             pltpu.SemaphoreType.DMA((2, half_devices)),
-            pltpu.SemaphoreType.DMA((half_devices,)),
         ],
         compiler_params=pltpu.CompilerParams(
-            vmem_limit_bytes=56 << 20, collective_id=0, has_side_effects=True
+            vmem_limit_bytes=60 << 20, collective_id=0, has_side_effects=True
         ),
         cost_estimate=pl.CostEstimate(
-            flops=experts * 2 * width * FF * 600, bytes_accessed=2 * tokens * width, transcendentals=0
+            flops=experts * width * FF * 600, bytes_accessed=2 * tokens * width, transcendentals=0
         ),
-    )(seeds, act, place)
+    )(seeds, *acts, place)
 
 
 def routing(meta, first_expert, group_size, capacity, tok_dev):
@@ -437,14 +468,21 @@
     x = jnp.dot(
         pick.reshape(EXP_DEV * slots, -1), every, preferred_element_type=jnp.float32
     ).astype(jnp.bfloat16).reshape(EXP_DEV, slots, -1)
-    act = run_up(expert_seeds, x, share, gate_w, up_w)
+    swap = [(rep, rep ^ 1) for rep in range(lax.axis_size("rep"))]
+    tiles = FF // COLS
+    act_main = run_up(expert_seeds, x, share, gate_w, up_w, 0, tiles - 1)
+    other_main = lax.ppermute(act_main, "rep", swap)
+    act_rest = run_up(expert_seeds, x, share, gate_w, up_w, tiles - 1, 1)
+    other_rest = lax.ppermute(act_rest, "rep", swap)
     nodes = devices_all // local_count
     if pairs_along_node(nodes, local_count):
         place = place.reshape(nodes // 2, 2, local_count, tok_dev, -1).transpose(1, 0, 2, 3, 4)
     else:
         place = place.reshape(nodes, local_count // 2, 2, tok_dev, -1).transpose(2, 0, 1, 3, 4)
     place = place.reshape(devices_all * tok_dev, -1)
-    return run_down(expert_seeds, act, place, tok_dev, width, nodes, local_count)
+    place = jnp.stack([place, lax.ppermute(place, "rep", swap)])
+    acts = (act_main, act_rest, other_main, other_rest)
+    return run_down(expert_seeds, acts, place, tok_dev, width, nodes, local_count)
 
 
 def solution(mesh):

time: 228 us -> 230 us (level)
  Pallas kernels: 192 us -> 179 us
  waiting for transfers between devices: 0.18 us -> 9.98 us
  starting transfers between devices: 0.01 us -> 5.09 us
    pallas_call x1, Pallas kernels: 73.7 us -> 56.7 us  [run_down(): pl.pallas_call(functools.partial(down_kernel, nodes, locals_), grid=(tile...]
    ppermute x0 -> x3, waiting for transfers between devices: none -> 9.81 us  [the longest x1 6.1 us: on_device(): place = jnp.stack([place, lax.ppermute(place, 'rep', swap)])]
    ppermute x0 -> x3, starting transfers between devices: none -> 5.09 us  [the longest x1 2.93 us: on_device(): other_main = lax.ppermute(act_main, 'rep', swap)]
    pallas_call x1 -> x2, Pallas kernels: 65.3 us -> 69.4 us  [run_up(): pl.pallas_call(functools.partial(up_kernel, first), grid=(half, count), i...]
  transfers between devices with their start and end apart: 1 -> 4, of which waited for: 1 -> 3; matrix products, arithmetic and copies ran while one was open for 0% -> 1% of each run, Pallas kernels for 23% -> 31%
where the time goes in v5:
time: 230 us
  Pallas kernels  179 us (78%)
  between operations  13.6 us (6%)
  waiting for transfers between devices  9.98 us (4%)
  matrix products  9.55 us (4%)
  local copies, waits for them, and re-layouts  6.86 us (3%)
  other arithmetic  6.17 us (3%)
  starting transfers between devices  5.09 us (2%)
    pallas_call x2, Pallas kernels, run_up(): pl.pallas_call(functools.partial(up_kernel, first), grid=(half, count), i...  69.4 us
    pallas_call x1, Pallas kernels, run_down(): pl.pallas_call(functools.partial(down_kernel, nodes, locals_), grid=(tile...  56.7 us
    pallas_call x1, Pallas kernels, make_weights(): pl.pallas_call(make_kernel, grid=(AHEAD, FF // COLS), in_specs=[pl.BlockS...  52.5 us
    dot_general x1, matrix products, on_device(): jnp.dot(pick.reshape(EXP_DEV * slots, -1), every, preferred_element_type=...  9.35 us
    ppermute x1, waiting for transfers between devices, on_device(): place = jnp.stack([place, lax.ppermute(place, 'rep', swap)])  6.1 us
  transfers between devices with their start and end apart: 4, of which 3 were waited for; matrix products, arithmetic and copies ran while one was open for 1% of the time, Pallas kernels for 31%

profile of v5, /device:TPU:0, one launch (start us, length us, event | category | flops | bytes accessed | tf_op | source)
XLA Modules:
  0.0 229.9 jit_solution(6751459512569106717)
XLA Ops:
  6.5 0.0 all-gather.2.cloned.1.call-start
  6.5 0.7 convert.12
  7.2 0.7 convert.11
  7.9 0.7 convert.10
  8.6 0.1 copy.29
  8.7 2.2 fusion.2
  10.9 0.0 all-gather.2.cloned.1.call-update
  11.0 0.0 copy-start.2
  11.0 0.6 copy-done.2
  11.6 52.5 %shard_map.55 = (bf16[2,7168,1024]{2,1,0:T(8,128)(2,1)}, bf16[2,7168,1024]{2,1,0:T(8,128)(2,1)}) custom-call(s32[4]{0:T(128)S(1)} %copy-done.2), custom_call_target="tpu_custom_call" | custom-call | flops 17616076800 | bytes 58720256 | tf_op jit(solution)/shard_map/pallas_call | solution.py:84
  64.1 0.2 all-gather.2.cloned.1.call-done
  64.3 0.9 slice.16
  65.2 0.1 copy.36
  65.4 0.1 fusion.4
  65.5 0.1 reshape.71
  65.6 0.2 fusion.1
  65.8 0.1 convert_element_type.33
  65.9 0.1 select_reduce_fusion.1
  66.0 0.1 copy.33
  66.2 0.2 bitcast_compare_fusion
  66.4 0.2 select_reduce_fusion
  66.6 0.1 copy.31.share
  66.7 0.0 copy-start.3
  66.8 9.4 %convolution_convert_fusion = bf16[512,7296]{1,0:T(8,128)(2,1)} fusion(pred[512,512]{1,0:T(32,128)(4,1)S(1)} %bitcast_compare_fusion, bf16[512,7296]{1,0:T(8,128)(2,1)} %all-gather.2.cloned.1.call-done), kind=kOutput, calls=%fused_computation | convolution fusion | flops 3828940800 | bytes 15204352 | tf_op jit(solution)/shard_map/dot_general | solution.py:468
  76.1 0.0 copy-done.3
  76.1 50.0 %shard_map.56 = bf16[2,2,128,768]{3,2,1,0:T(8,128)(2,1)S(1)} custom-call(s32[4]{0:T(128)S(1)} %copy-done.3, bf16[2,2,128,7296]{3,2,1,0:T(8,128)(2,1)} %bitcast.31, f32[2,2,128,1]{3,2,1,0:T(8,128)S(1)} %copy.31.share, bf16[2,7168,1024]{2,1,0:T(8,128)(2,1)} %get-tuple-element.7.gate_w, bf16[2,7168,1024]{2,1,0:T(8,128)(2,1)} %get-tuple-element.8.up_w), custom_call_target="tpu_custom_call" | custom-call | flops 13212057600 | bytes 7471104 | tf_op jit(solution)/shard_map/pallas_call | solution.py:150
  126.1 0.0 copy-start
  126.1 2.9 %collective-permute-start = (bf16[4,128,768]{2,1,0:T(8,128)(2,1)S(1)}, bf16[4,128,768]{2,1,0:T(8,128)(2,1)}, u32[]{:S(2)}, u32[]{:S(2)}) collective-permute-start(bf16[4,128,768]{2,1,0:T(8,128)(2,1)S(1)} %bitcast.27), channel_id=1, source_target_pairs={{0,8},{8,0},{16,24},{24,16},{1,9},{9,1},{17,25},{25,17},{2,10},{10... | collective-permute-start | bytes 2359304 | tf_op jit(solution)/shard_map/ppermute | solution.py:474
  129.1 1.3 eq.84
  130.4 0.4 eq.85
  130.8 0.1 fusion.3
  131.0 0.1 collective-permute-start.2
  131.1 19.4 %shard_map.57 = bf16[2,2,128,256]{3,2,1,0:T(8,128)(2,1)S(1)} custom-call(s32[4]{0:T(128)S(1)} %copy-done.3, bf16[2,2,128,7296]{3,2,1,0:T(8,128)(2,1)} %bitcast.32, f32[2,2,128,1]{3,2,1,0:T(8,128)S(1)} %copy.31.share, bf16[2,7168,1024]{2,1,0:T(8,128)(2,1)} %get-tuple-element.7.gate_w, bf16[2,7168,1024]{2,1,0:T(8,128)(2,1)} %get-tuple-element.8.up_w), custom_call_target="tpu_custom_call" | custom-call | flops 4404019200 | bytes 7471104 | tf_op jit(solution)/shard_map/pallas_call | solution.py:150
  150.5 0.0 copy-done
  150.5 0.0 copy-start.1
  150.5 2.1 collective-permute-start.1
  152.6 6.1 %collective-permute-done.2 = bf16[512,512]{1,0:T(8,128)(2,1)S(1)} collective-permute-done((bf16[512,512]{1,0:T(8,128)(2,1)S(1)}, bf16[512,512]{1,0:T(8,128)(2,1)S(1)}, u32[]{:S(2)}, u32[]{:S(2)}) %collective-permute-start.2) | collective-permute-done | bytes 524320 | tf_op jit(solution)/shard_map/ppermute | solution.py:483
  158.7 1.1 pad_maximum_fusion.place
  159.8 3.7 %collective-permute-done.1.other_rest = bf16[4,128,256]{2,1,0:T(8,128)(2,1)S(1)} collective-permute-done((bf16[4,128,256]{2,1,0:T(8,128)(2,1)S(1)}, bf16[4,128,256]{2,1,0:T(8,128)(2,1)S(1)}, u32[]{:S(2)}, u32[]{:S(2)}) %collective-permute-start.1) | collective-permute-done | bytes 262176 | tf_op jit(solution)/shard_map/ppermute | solution.py:476
  163.5 0.0 copy-start.4
  163.5 0.0 collective-permute-done.other_main
  163.5 0.0 copy-done.1
  163.5 0.7 copy-done.4
  164.2 56.7 %shard_map.58 = bf16[64,7168]{1,0:T(8,128)(2,1)} custom-call(s32[4]{0:T(128)} %seeds.7, bf16[4,128,768]{2,1,0:T(8,128)(2,1)} %bitcast.28, bf16[4,128,256]{2,1,0:T(8,128)(2,1)} %bitcast.30, bf16[4,128,768]{2,1,0:T(8,128)(2,1)} %collective-permute-done.other_main, bf16[4,128,256]{2,1,0:T(8,128)(2,1)} %copy-done.4, bf16[2,512,512]{2,1,0:T(8,128)(2,1)} %pad_maximum_fusion.place), custom_call_target="tpu_custom_call" | custom-call | flops 17616076800 | bytes 7340032 | tf_op jit(solution)/shard_map/pallas_call | solution.py:386
  220.9 2.2 copy.40
  (13 shorter events, 0.2 us)
Async XLA Ops:
  6.5 57.8 %all-gather.2.cloned.1.call-start = ((), (), s32[]{:S(2)}) async-start(), calls=%async_computation | async-start | bytes 8404992 | tf_op jit(solution)/shard_map/all_gather | solution.py:457
  11.0 0.7 copy-start.2
  66.7 9.4 %copy-start.3 = (s32[4]{0:T(128)S(1)}, s32[4]{0:T(128)}, u32[]{:S(2)}) copy-start(s32[4]{0:T(128)} %seeds.7) | copy-start | bytes 52
  126.1 24.4 %copy-start = (bf16[2,2,128,768]{3,2,1,0:T(8,128)(2,1)}, bf16[2,2,128,768]{3,2,1,0:T(8,128)(2,1)S(1)}, u32[]{:S(2)}) copy-start(bf16[2,2,128,768]{3,2,1,0:T(8,128)(2,1)S(1)} %shard_map.56) | copy-start | bytes 2359300
  126.1 37.3 %collective-permute-start = (bf16[4,128,768]{2,1,0:T(8,128)(2,1)S(1)}, bf16[4,128,768]{2,1,0:T(8,128)(2,1)}, u32[]{:S(2)}, u32[]{:S(2)}) collective-permute-start(bf16[4,128,768]{2,1,0:T(8,128)(2,1)S(1)} %bitcast.27), channel_id=1, source_target_pairs={{0,8},{8,0},{16,24},{24,16},{1,9},{9,1},{17,25},{25,17},{2,10},{10... | collective-permute-start | bytes 2359304 | tf_op jit(solution)/shard_map/ppermute | solution.py:474
  131.0 27.7 %collective-permute-start.2 = (bf16[512,512]{1,0:T(8,128)(2,1)S(1)}, bf16[512,512]{1,0:T(8,128)(2,1)S(1)}, u32[]{:S(2)}, u32[]{:S(2)}) collective-permute-start(bf16[512,512]{1,0:T(8,128)(2,1)S(1)} %bitcast.33), channel_id=1, source_target_pairs={{0,8},{8,0},{16,24},{24,16},{1,9},{9,1},{17,25},{25,17},{2,10},{10... | collective-permute-start | bytes 1572872 | tf_op jit(solution)/shard_map/ppermute | solution.py:483
  150.5 13.0 %copy-start.1 = (bf16[2,2,128,256]{3,2,1,0:T(8,128)(2,1)}, bf16[2,2,128,256]{3,2,1,0:T(8,128)(2,1)S(1)}, u32[]{:S(2)}) copy-start(bf16[2,2,128,256]{3,2,1,0:T(8,128)(2,1)S(1)} %shard_map.57) | copy-start | bytes 786436
  150.5 12.9 %collective-permute-start.1 = (bf16[4,128,256]{2,1,0:T(8,128)(2,1)S(1)}, bf16[4,128,256]{2,1,0:T(8,128)(2,1)S(1)}, u32[]{:S(2)}, u32[]{:S(2)}) collective-permute-start(bf16[4,128,256]{2,1,0:T(8,128)(2,1)S(1)} %bitcast.29), channel_id=1, source_target_pairs={{0,8},{8,0},{16,24},{24,16},{1,9},{9,1},{17,25},{25,17},{2,10},{10... | collective-permute-start | bytes 786440 | tf_op jit(solution)/shard_map/ppermute | solution.py:476
  163.5 0.7 copy-start.4
Sparse Core Ops, SparseCore 0:
  11.0 53.1 all-gather.1

commit v6 on v5

--- a/solution.py
+++ b/solution.py
@@ -26,7 +26,7 @@
 ROWS = 512
 COLS = 256
 PIECE = 64
-DOWN_COLS = 512
+DOWN_COLS = 256
 AHEAD = 2
 META = 128
 
@@ -181,7 +181,7 @@
     pair_send, pair_recv, push_send, push_recv,
 ):
     step_now = pl.program_id(0)
-    tiles = pl.num_programs(0) - 2
+    tiles = pl.num_programs(0) - 1
     experts, slots, main = act_main.shape
     tok_dev, width = out.shape
     part_width = width // 2
@@ -196,7 +196,6 @@
     halves = DOWN_COLS // COLS
     units = experts * halves
     done = step_now - 1
-    onward = step_now - 2
     slot = lax.rem(step_now, 2)
 
     def device(index):
@@ -301,56 +300,61 @@
     def _():
         pl.semaphore_wait(barrier, 2 * half_devices)
 
-    @pl.when(step_now >= 4)
-    def _():
-        each_target(lambda which, step: push(which, step, slot, onward - 2).wait_send())
-
-    @pl.when(step_now >= 2)
-    def _():
-        pair_copy(1 - slot, onward).wait_recv()
+    @pl.when(step_now >= 3)
+    def _():
+        pair_copy(slot, done - 2).wait_send()
+
+    @pl.when(step_now < tiles)
+    def _():
+        combine()
+        make(step_now, 1)
+        use(0)
+
+    @pl.when(step_now == tiles)
+    def _():
+        combine()
+
+    @pl.when(step_now >= 1)
+    def _():
+        pair_copy(slot, done).start()
+
+    def run_units(first, last):
+        @pl.when(step_now < tiles)
+        def _():
+            for unit in range(first, last):
+                make(step_now + (unit + 1) // units, (unit + 1) % units)
+                use(unit)
+
+    run_units(1, units - 1)
+
+    @pl.when(step_now >= 3)
+    def _():
+        each_target(lambda which, step: push(which, step, slot, done - 2).wait_send())
+
+    @pl.when(step_now >= 1)
+    def _():
+        pair_copy(slot, done).wait_recv()
 
         @pl.loop(0, half_devices)
         def _(index):
             for which in range(2):
-                mine = sent[1 - slot, side, which, block(index), :].astype(jnp.float32)
-                theirs = paired[which, block(index), columns(onward)].astype(jnp.float32)
+                mine = sent[slot, side, which, block(index), :].astype(jnp.float32)
+                theirs = paired[which, block(index), columns(done)].astype(jnp.float32)
                 pushed[slot, which, block(index), :] = (mine + theirs).astype(jnp.bfloat16)
 
-        each_target(lambda which, step: push(which, step, slot, onward).start())
-        arrived[0, me, :, columns(onward)] = pushed[slot, 0, block(me), :]
-
-    @pl.when((step_now >= 3) & (step_now <= tiles))
-    def _():
-        pair_copy(slot, done - 2).wait_send()
-
-    @pl.when(step_now < tiles)
-    def _():
-        combine()
-        make(step_now, 1)
-        use(0)
+        each_target(lambda which, step: push(which, step, slot, done).start())
+        arrived[0, me, :, columns(done)] = pushed[slot, 0, block(me), :]
+
+    run_units(units - 1, units)
 
     @pl.when(step_now == tiles)
     def _():
-        combine()
-
-    @pl.when((step_now >= 1) & (step_now <= tiles))
-    def _():
-        pair_copy(slot, done).start()
-
-    @pl.when(step_now < tiles)
-    def _():
-        for unit in range(1, units):
-            make(step_now + (unit + 1) // units, (unit + 1) % units)
-            use(unit)
-
-    @pl.when(step_now == tiles + 1)
-    def _():
-        pair_copy(slot, tiles - 2).wait_send()
-        pair_copy(1 - slot, tiles - 1).wait_send()
+        pair_copy(1 - slot, tiles - 2).wait_send()
+        pair_copy(slot, tiles - 1).wait_send()
 
         def finish(which, step):
-            push(which, step, 1 - slot, onward - 1).wait_send()
-            push(which, step, slot, onward).wait_send()
+            push(which, step, 1 - slot, done - 1).wait_send()
+            push(which, step, slot, done).wait_send()
             source = peer(step)
             pltpu.make_async_remote_copy(
                 src_ref=arrived.at[which, source],
@@ -385,7 +389,7 @@
     tokens = place.shape[1]
     return pl.pallas_call(
         functools.partial(down_kernel, nodes, locals_),
-        grid=(tiles + 2,),
+        grid=(tiles + 1,),
         in_specs=[
             pl.BlockSpec(memory_space=pltpu.SMEM),
             *[pl.BlockSpec(act.shape, lambda t: (0, 0, 0)) for act in acts],
@@ -438,10 +442,9 @@
     source = (jnp.arange(total, dtype=jnp.int32) // tok_dev)[:, None]
     slot = jnp.where(hit & (rank < capacity), source * capacity + rank, -1)
     slots = jnp.arange(sources * capacity, dtype=jnp.int32)
-    place = (slot[:, :, None] == slots).astype(jnp.bfloat16).reshape(total, -1)
     pick = slot.T[:, None, :] == slots[None, :, None]
     slot_share = jnp.sum(jnp.where(pick, share.T[:, None, :], 0.0), axis=2, keepdims=True)
-    return pick.astype(jnp.bfloat16), place, slot_share
+    return pick.astype(jnp.bfloat16), slot, slot_share
 
 
 def on_device(tokens, expert_ids, node_groups, gate_levels, expert_seeds):
@@ -456,7 +459,7 @@
     meta = jnp.pad(meta, ((0, 0), (0, META - meta.shape[1])))
     every = lax.all_gather(jnp.concatenate([tokens, meta], axis=1), AXES, axis=0, tiled=True)
     gate_w, up_w = make_weights(expert_seeds)
-    pick, place, share = routing(
+    pick, slot, share = routing(
         every[:, width : width + 2 * TOP + node_groups.shape[1]].astype(jnp.int32),
         me * EXP_DEV,
         EXP_DEV * local_count,
@@ -464,23 +467,27 @@
         tok_dev,
     )
 
+    swap = [(rep, rep ^ 1) for rep in range(lax.axis_size("rep"))]
+    nodes = devices_all // local_count
+    if pairs_along_node(nodes, local_count):
+        slot = slot.reshape(nodes // 2, 2, local_count, tok_dev, -1).transpose(1, 0, 2, 3, 4)
+    else:
+        slot = slot.reshape(nodes, local_count // 2, 2, tok_dev, -1).transpose(2, 0, 1, 3, 4)
+    slot = slot.reshape(devices_all * tok_dev, -1)
+    slot = jnp.stack([slot, lax.ppermute(slot, "rep", swap)])
+    place = (slot[..., None] == jnp.arange(pick.shape[1], dtype=jnp.int32)).astype(jnp.bfloat16)
+    place = place.reshape(2, devices_all * tok_dev, -1)
+
     slots = pick.shape[1]
     x = jnp.dot(
         pick.reshape(EXP_DEV * slots, -1), every, preferred_element_type=jnp.float32
     ).astype(jnp.bfloat16).reshape(EXP_DEV, slots, -1)
-    swap = [(rep, rep ^ 1) for rep in range(lax.axis_size("rep"))]
     tiles = FF // COLS
     act_main = run_up(expert_seeds, x, share, gate_w, up_w, 0, tiles - 1)
     other_main = lax.ppermute(act_main, "rep", swap)
+    share, place = lax.optimization_barrier((share, place))
     act_rest = run_up(expert_seeds, x, share, gate_w, up_w, tiles - 1, 1)
     other_rest = lax.ppermute(act_rest, "rep", swap)
-    nodes = devices_all // local_count
-    if pairs_along_node(nodes, local_count):
-        place = place.reshape(nodes // 2, 2, local_count, tok_dev, -1).transpose(1, 0, 2, 3, 4)
-    else:
-        place = place.reshape(nodes, local_count // 2, 2, tok_dev, -1).transpose(2, 0, 1, 3, 4)
-    place = place.reshape(devices_all * tok_dev, -1)
-    place = jnp.stack([place, lax.ppermute(place, "rep", swap)])
     acts = (act_main, act_rest, other_main, other_rest)
     return run_down(expert_seeds, acts, place, tok_dev, width, nodes, local_count)
 

time: 230 us -> 229 us (level)
  waiting for transfers between devices: 9.98 us -> 5.93 us
  local copies, waits for them, and re-layouts: 6.86 us -> 10.3 us
    ppermute x1, waiting for transfers between devices: 6.1 us -> 0.01 us  [on_device(): slot = jnp.stack([slot, lax.ppermute(slot, 'rep', swap)])]
    eq x2, local copies, waits for them, and re-layouts: 1.71 us -> 4.69 us  [on_device(): slot[..., None] == jnp.arange(pick.shape[1], dtype=jnp.int32)]
    ppermute x1, starting transfers between devices: 2.93 us -> 0.02 us  [on_device(): other_main = lax.ppermute(act_main, 'rep', swap)]
    convert_element_type x0 -> x1, other arithmetic: none -> 2.88 us  [on_device(): (slot[..., None] == jnp.arange(pick.shape[1], dtype=jnp.int32)).astype(jn...]
    ppermute x1, starting transfers between devices: 0.1 us -> 2.88 us  [on_device(): slot = jnp.stack([slot, lax.ppermute(slot, 'rep', swap)])]
  transfers between devices with their start and end apart: 4 -> 4, of which waited for: 3 -> 2; matrix products, arithmetic and copies ran while one was open for 1% -> 8% of each run, Pallas kernels for 31% -> 53%
where the time goes in v6:
time: 229 us
  Pallas kernels  177 us (77%)
  between operations  13.6 us (6%)
  local copies, waits for them, and re-layouts  10.3 us (4%)
  matrix products  9.46 us (4%)
  other arithmetic  7.88 us (3%)
  waiting for transfers between devices  5.93 us (3%)
  starting transfers between devices  4.97 us (2%)
    pallas_call x2, Pallas kernels, run_up(): pl.pallas_call(functools.partial(up_kernel, first), grid=(half, count), i...  69.5 us
    pallas_call x1, Pallas kernels, run_down(): pl.pallas_call(functools.partial(down_kernel, nodes, locals_), grid=(tile...  54.6 us
    pallas_call x1, Pallas kernels, make_weights(): pl.pallas_call(make_kernel, grid=(AHEAD, FF // COLS), in_specs=[pl.BlockS...  52.5 us
    dot_general x1, matrix products, on_device(): jnp.dot(pick.reshape(EXP_DEV * slots, -1), every, preferred_element_type=...  9.26 us
    ppermute x1, waiting for transfers between devices, on_device(): other_rest = lax.ppermute(act_rest, 'rep', swap)  5.77 us
    eq x2, local copies, waits for them, and re-layouts, on_device(): slot[..., None] == jnp.arange(pick.shape[1], dtype=jnp.int32)  4.69 us
  transfers between devices with their start and end apart: 4, of which 2 were waited for; matrix products, arithmetic and copies ran while one was open for 8% of the time, Pallas kernels for 53%

profile of v6, /device:TPU:0, one launch (start us, length us, event | category | flops | bytes accessed | tf_op | source)
XLA Modules:
  0.0 228.7 jit_solution(12784133389663801075)
XLA Ops:
  6.5 0.0 all-gather.2.cloned.1.call-start
  6.5 0.7 convert.11
  7.2 0.7 convert.9
  7.9 0.7 convert.10
  8.6 0.1 copy.28
  8.7 2.2 fusion.1
  10.9 0.0 all-gather.2.cloned.1.call-update
  11.0 0.0 copy-start.2
  11.0 0.6 copy-done.2
  11.7 52.5 %shard_map.55 = (bf16[2,7168,1024]{2,1,0:T(8,128)(2,1)}, bf16[2,7168,1024]{2,1,0:T(8,128)(2,1)}) custom-call(s32[4]{0:T(128)S(1)} %copy-done.2), custom_call_target="tpu_custom_call" | custom-call | flops 17616076800 | bytes 58720256 | tf_op jit(solution)/shard_map/pallas_call | solution.py:84
  64.2 0.1 all-gather.2.cloned.1.call-done
  64.3 0.9 slice.16
  65.2 0.1 copy.35
  65.4 0.1 fusion.2
  65.5 0.1 reshape.63
  65.6 0.1 reduce_or.22
  65.7 0.1 select_reduce_fusion.1
  65.8 0.2 convolution_convert_fusion.1
  66.1 0.1 reshape.65
  66.2 0.1 convert_element_type.36
  66.2 2.9 %collective-permute-start = (s32[512,4]{0,1:T(4,128)S(1)}, s32[512,4]{0,1:T(4,128)S(1)}, u32[]{:S(2)}, u32[]{:S(2)}) collective-permute-start(s32[512,4]{0,1:T(4,128)S(1)} %reshape.65), channel_id=1, source_target_pairs={{0,8},{8,0},{16,24},{24,16},{1,9},{9,1},{17,25},{25,17},{2,10},{10... | collective-permute-start | bytes 24584 | tf_op jit(solution)/shard_map/ppermute | solution.py:477
  69.1 0.2 select_reduce_fusion
  69.3 0.2 bitcast_compare_fusion
  69.5 0.1 copy.30.share
  69.7 0.0 copy-start.3
  69.7 9.3 %convolution_convert_fusion = bf16[512,7296]{1,0:T(8,128)(2,1)} fusion(pred[512,512]{1,0:T(32,128)(4,1)S(1)} %bitcast_compare_fusion, bf16[512,7296]{1,0:T(8,128)(2,1)} %all-gather.2.cloned.1.call-done), kind=kOutput, calls=%fused_computation | convolution fusion | flops 3828940800 | bytes 15204352 | tf_op jit(solution)/shard_map/dot_general | solution.py:482
  79.0 0.0 copy-done.3
  79.0 50.0 %shard_map.56 = bf16[2,2,128,768]{3,2,1,0:T(8,128)(2,1)S(1)} custom-call(s32[4]{0:T(128)S(1)} %copy-done.3, bf16[2,2,128,7296]{3,2,1,0:T(8,128)(2,1)} %bitcast.39, f32[2,2,128,1]{3,2,1,0:T(8,128)S(1)} %copy.30.share, bf16[2,7168,1024]{2,1,0:T(8,128)(2,1)} %get-tuple-element.9.gate_w, bf16[2,7168,1024]{2,1,0:T(8,128)(2,1)} %get-tuple-element.10.up_w), custom_call_target="tpu_custom_call" | custom-call | flops 13212057600 | bytes 7471104 | tf_op jit(solution)/shard_map/pallas_call | solution.py:150
  129.0 0.0 copy-start
  129.0 0.1 stack_reshape.3
  129.1 0.0 collective-permute-start.1
  129.1 0.0 collective-permute-done
  129.1 0.2 copy.33
  129.4 2.9 %eq.84 = s32[2,512,4,128]{3,2,1,0:T(4,128)S(1)} broadcast(s32[2,512,4]{2,1,0:T(8,128)S(1)} %copy.33), dimensions={0,1,2} | broadcast | bytes 2113536 | tf_op jit(solution)/shard_map/eq | solution.py:478
  132.2 1.8 eq.85
  134.1 2.9 %compare_convert_fusion.place = bf16[2,512,512]{2,1,0:T(8,128)(2,1)} fusion(s32[2,512,512]{2,1,0:T(8,128)} %eq.85, s32[512]{0:T(512)S(1)} %iota_bitcast_fusion), kind=kLoop, calls=%fused_computation.1 | loop fusion | flops 1048576 | bytes 3147776 | tf_op jit(solution)/shard_map/convert_element_type | solution.py:478
  136.9 0.1 copy.34.share
  137.1 19.4 %shard_map.57 = bf16[2,2,128,256]{3,2,1,0:T(8,128)(2,1)S(1)} custom-call(s32[4]{0:T(128)S(1)} %copy-done.3, bf16[2,2,128,7296]{3,2,1,0:T(8,128)(2,1)} %bitcast.40, f32[2,2,128,1]{3,2,1,0:T(8,128)S(1)} %copy.34.share, bf16[2,7168,1024]{2,1,0:T(8,128)(2,1)} %get-tuple-element.9.gate_w, bf16[2,7168,1024]{2,1,0:T(8,128)(2,1)} %get-tuple-element.10.up_w), custom_call_target="tpu_custom_call" | custom-call | flops 4404019200 | bytes 7471104 | tf_op jit(solution)/shard_map/pallas_call | solution.py:150
  156.5 0.0 copy-done
  156.5 0.0 copy-start.1
  156.6 2.1 collective-permute-start.2
  158.6 5.8 %collective-permute-done.2.other_rest = bf16[4,128,256]{2,1,0:T(8,128)(2,1)S(1)} collective-permute-done((bf16[4,128,256]{2,1,0:T(8,128)(2,1)S(1)}, bf16[4,128,256]{2,1,0:T(8,128)(2,1)S(1)}, u32[]{:S(2)}, u32[]{:S(2)}) %collective-permute-start.2) | collective-permute-done | bytes 262176 | tf_op jit(solution)/shard_map/ppermute | solution.py:490
  164.4 0.0 copy-start.4
  164.4 0.0 collective-permute-done.1.other_main
  164.4 0.0 copy-done.1
  164.4 0.7 copy-done.4
  165.1 54.6 %shard_map.58 = bf16[64,7168]{1,0:T(8,128)(2,1)} custom-call(s32[4]{0:T(128)} %seeds.7, bf16[4,128,768]{2,1,0:T(8,128)(2,1)} %bitcast.36, bf16[4,128,256]{2,1,0:T(8,128)(2,1)} %bitcast.38, bf16[4,128,768]{2,1,0:T(8,128)(2,1)} %collective-permute-done.1.other_main, bf16[4,128,256]{2,1,0:T(8,128)(2,1)} %copy-done.4, bf16[2,512,512]{2,1,0:T(8,128)(2,1)} %compare_convert_fusion.place), custom_call_target="tpu_custom_call" | custom-call | flops 17616076800 | bytes 7340032 | tf_op jit(solution)/shard_map/pallas_call | solution.py:390
  219.7 2.2 copy.39
  (16 shorter events, 0.2 us)
Async XLA Ops:
  6.5 57.8 %all-gather.2.cloned.1.call-start = ((), (), s32[]{:S(2)}) async-start(), calls=%async_computation | async-start | bytes 8404992 | tf_op jit(solution)/shard_map/all_gather | solution.py:460
  11.0 0.7 copy-start.2
  66.2 62.9 %collective-permute-start = (s32[512,4]{0,1:T(4,128)S(1)}, s32[512,4]{0,1:T(4,128)S(1)}, u32[]{:S(2)}, u32[]{:S(2)}) collective-permute-start(s32[512,4]{0,1:T(4,128)S(1)} %reshape.65), channel_id=1, source_target_pairs={{0,8},{8,0},{16,24},{24,16},{1,9},{9,1},{17,25},{25,17},{2,10},{10... | collective-permute-start | bytes 24584 | tf_op jit(solution)/shard_map/ppermute | solution.py:477
  69.7 9.3 %copy-start.3 = (s32[4]{0:T(128)S(1)}, s32[4]{0:T(128)}, u32[]{:S(2)}) copy-start(s32[4]{0:T(128)} %seeds.7) | copy-start | bytes 52
  129.0 27.6 %copy-start = (bf16[2,2,128,768]{3,2,1,0:T(8,128)(2,1)}, bf16[2,2,128,768]{3,2,1,0:T(8,128)(2,1)S(1)}, u32[]{:S(2)}) copy-start(bf16[2,2,128,768]{3,2,1,0:T(8,128)(2,1)S(1)} %shard_map.56) | copy-start | bytes 2359300
  129.1 35.3 %collective-permute-start.1 = (bf16[4,128,768]{2,1,0:T(8,128)(2,1)S(1)}, bf16[4,128,768]{2,1,0:T(8,128)(2,1)}, u32[]{:S(2)}, u32[]{:S(2)}) collective-permute-start(bf16[4,128,768]{2,1,0:T(8,128)(2,1)S(1)} %bitcast.35), channel_id=1, source_target_pairs={{0,8},{8,0},{16,24},{24,16},{1,9},{9,1},{17,25},{25,17},{2,10},{10... | collective-permute-start | bytes 2359304 | tf_op jit(solution)/shard_map/ppermute | solution.py:487
  156.5 7.8 %copy-start.1 = (bf16[2,2,128,256]{3,2,1,0:T(8,128)(2,1)}, bf16[2,2,128,256]{3,2,1,0:T(8,128)(2,1)S(1)}, u32[]{:S(2)}) copy-start(bf16[2,2,128,256]{3,2,1,0:T(8,128)(2,1)S(1)} %shard_map.57) | copy-start | bytes 786436
  156.6 7.8 %collective-permute-start.2 = (bf16[4,128,256]{2,1,0:T(8,128)(2,1)S(1)}, bf16[4,128,256]{2,1,0:T(8,128)(2,1)S(1)}, u32[]{:S(2)}, u32[]{:S(2)}) collective-permute-start(bf16[4,128,256]{2,1,0:T(8,128)(2,1)S(1)} %bitcast.37), channel_id=1, source_target_pairs={{0,8},{8,0},{16,24},{24,16},{1,9},{9,1},{17,25},{25,17},{2,10},{10... | collective-permute-start | bytes 786440 | tf_op jit(solution)/shard_map/ppermute | solution.py:490
  164.4 0.7 copy-start.4
Sparse Core Ops, SparseCore 0:
  11.1 53.2 all-gather.1

commit v7 on v6

--- a/solution.py
+++ b/solution.py
@@ -176,8 +176,8 @@
 
 
 def down_kernel(
-    nodes, locals_, seeds, act_main, act_rest, other_main, other_rest, place, out,
-    lin, made, y, sent, paired, pushed, arrived,
+    nodes, locals_, seeds, act_main, act_rest, other_main, other_rest, token_slot, out,
+    place, lin, made, y, sent, paired, pushed, arrived,
     pair_send, pair_recv, push_send, push_recv,
 ):
     step_now = pl.program_id(0)
@@ -293,6 +293,18 @@
         each_target(lambda which, step: greet(target(which, peer(step))))
 
         fill_index(lin, D)
+
+        @pl.loop(0, place.shape[1] // tok_dev)
+        def _(index):
+            number = lax.broadcasted_iota(jnp.int32, (tok_dev, slots), 1)
+            for which in range(2):
+                theirs = token_slot[which, block(index), :]
+                for expert in range(experts):
+                    hit = theirs[:, expert : expert + 1] == number
+                    place[which, block(index), expert * slots : (expert + 1) * slots] = jnp.where(
+                        hit, 1.0, 0.0
+                    ).astype(jnp.bfloat16)
+
         y[...] = jnp.zeros_like(y)
         make(0, 0)
 
@@ -382,22 +394,23 @@
                 out[:, span] = total.astype(jnp.bfloat16)
 
 
-def run_down(seeds, acts, place, tok_dev, width, nodes, locals_):
+def run_down(seeds, acts, slot, tok_dev, width, nodes, locals_):
     experts, slots, _ = acts[0].shape
     half_devices = nodes * locals_ // 2
     tiles = width // 2 // DOWN_COLS
-    tokens = place.shape[1]
+    tokens = slot.shape[1]
     return pl.pallas_call(
         functools.partial(down_kernel, nodes, locals_),
         grid=(tiles + 1,),
         in_specs=[
             pl.BlockSpec(memory_space=pltpu.SMEM),
             *[pl.BlockSpec(act.shape, lambda t: (0, 0, 0)) for act in acts],
-            pl.BlockSpec(place.shape, lambda t: (0, 0, 0)),
+            pl.BlockSpec(slot.shape, lambda t: (0, 0, 0)),
         ],
         out_specs=pl.BlockSpec((tok_dev, width), lambda t: (0, 0)),
         out_shape=jax.ShapeDtypeStruct((tok_dev, width), jnp.bfloat16),
         scratch_shapes=[
+            pltpu.VMEM((2, tokens, experts * slots), jnp.bfloat16),
             pltpu.VMEM((PIECE, COLS), jnp.int32),
             pltpu.VMEM((2, FF, COLS), jnp.bfloat16),
             pltpu.VMEM((2, experts * slots, DOWN_COLS), jnp.bfloat16),
@@ -416,7 +429,7 @@
         cost_estimate=pl.CostEstimate(
             flops=experts * width * FF * 600, bytes_accessed=2 * tokens * width, transcendentals=0
         ),
-    )(seeds, *acts, place)
+    )(seeds, *acts, slot)
 
 
 def routing(meta, first_expert, group_size, capacity, tok_dev):
@@ -475,8 +488,6 @@
         slot = slot.reshape(nodes, local_count // 2, 2, tok_dev, -1).transpose(2, 0, 1, 3, 4)
     slot = slot.reshape(devices_all * tok_dev, -1)
     slot = jnp.stack([slot, lax.ppermute(slot, "rep", swap)])
-    place = (slot[..., None] == jnp.arange(pick.shape[1], dtype=jnp.int32)).astype(jnp.bfloat16)
-    place = place.reshape(2, devices_all * tok_dev, -1)
 
     slots = pick.shape[1]
     x = jnp.dot(
@@ -485,11 +496,10 @@
     tiles = FF // COLS
     act_main = run_up(expert_seeds, x, share, gate_w, up_w, 0, tiles - 1)
     other_main = lax.ppermute(act_main, "rep", swap)
-    share, place = lax.optimization_barrier((share, place))
     act_rest = run_up(expert_seeds, x, share, gate_w, up_w, tiles - 1, 1)
     other_rest = lax.ppermute(act_rest, "rep", swap)
     acts = (act_main, act_rest, other_main, other_rest)
-    return run_down(expert_seeds, acts, place, tok_dev, width, nodes, local_count)
+    return run_down(expert_seeds, acts, slot, tok_dev, width, nodes, local_count)
 
 
 def solution(mesh):

time: 229 us -> 223 us (0.974)
  local copies, waits for them, and re-layouts: 10.3 us -> 7.18 us
  other arithmetic: 7.88 us -> 4.99 us
    ppermute x1, waiting for transfers between devices: 5.77 us -> 0.01 us  [on_device(): other_rest = lax.ppermute(act_rest, 'rep', swap)]
    ppermute x1, waiting for transfers between devices: 0.01 us -> 5.69 us  [on_device(): slot = jnp.stack([slot, lax.ppermute(slot, 'rep', swap)])]
    eq x2 -> x0, local copies, waits for them, and re-layouts: 4.69 us -> none  [on_device(): slot[..., None] == jnp.arange(pick.shape[1], dtype=jnp.int32)]
    ppermute x1, starting transfers between devices: 0.02 us -> 2.94 us  [on_device(): other_main = lax.ppermute(act_main, 'rep', swap)]
    convert_element_type x1 -> x0, other arithmetic: 2.88 us -> none  [on_device(): (slot[..., None] == jnp.arange(pick.shape[1], dtype=jnp.int32)).astype(jn...]
  transfers between devices with their start and end apart: 4 -> 4, of which waited for: 2 -> 2; matrix products, arithmetic and copies ran while one was open for 8% -> 1% of each run, Pallas kernels for 53% -> 32%
where the time goes in v7:
time: 223 us
  Pallas kernels  177 us (79%)
  between operations  13.6 us (6%)
  matrix products  9.54 us (4%)
  local copies, waits for them, and re-layouts  7.18 us (3%)
  waiting for transfers between devices  5.87 us (3%)
  starting transfers between devices  5.03 us (2%)
  other arithmetic  4.99 us (2%)
    pallas_call x2, Pallas kernels, run_up(): pl.pallas_call(functools.partial(up_kernel, first), grid=(half, count), i...  69.4 us
    pallas_call x1, Pallas kernels, run_down(): pl.pallas_call(functools.partial(down_kernel, nodes, locals_), grid=(tile...  54.7 us
    pallas_call x1, Pallas kernels, make_weights(): pl.pallas_call(make_kernel, grid=(AHEAD, FF // COLS), in_specs=[pl.BlockS...  52.5 us
    dot_general x1, matrix products, on_device(): jnp.dot(pick.reshape(EXP_DEV * slots, -1), every, preferred_element_type=...  9.34 us
    ppermute x1, waiting for transfers between devices, on_device(): slot = jnp.stack([slot, lax.ppermute(slot, 'rep', swap)])  5.69 us
    unnamed x14, local copies, waits for them, and re-layouts  4.53 us
  transfers between devices with their start and end apart: 4, of which 2 were waited for; matrix products, arithmetic and copies ran while one was open for 1% of the time, Pallas kernels for 32%

profile of v7, /device:TPU:0, one launch (start us, length us, event | category | flops | bytes accessed | tf_op | source)
XLA Modules:
  0.0 222.8 jit_solution(13452103442595296698)
XLA Ops:
  6.5 0.0 all-gather.2.cloned.1.call-start
  6.5 0.7 convert.11
  7.2 0.7 convert.10
  7.9 0.7 convert.9
  8.6 0.1 copy.39
  8.7 2.2 fusion.1
  10.9 0.0 all-gather.2.cloned.1.call-update
  11.0 0.0 copy-start.2
  11.0 0.6 copy-done.2
  11.6 52.5 %shard_map.55 = (bf16[2,7168,1024]{2,1,0:T(8,128)(2,1)}, bf16[2,7168,1024]{2,1,0:T(8,128)(2,1)}) custom-call(s32[4]{0:T(128)S(1)} %copy-done.2), custom_call_target="tpu_custom_call" | custom-call | flops 17616076800 | bytes 58720256 | tf_op jit(solution)/shard_map/pallas_call | solution.py:84
  64.1 0.2 all-gather.2.cloned.1.call-done
  64.3 0.9 slice.16
  65.2 0.1 copy.46
  65.4 0.1 fusion.2
  65.5 0.1 reshape.56
  65.6 0.2 convolution_convert_fusion.1
  65.8 0.1 convert_element_type.32
  65.9 0.1 select_reduce_fusion.1
  66.0 0.2 bitcast_compare_fusion
  66.2 0.2 select_reduce_fusion
  66.4 0.1 copy.41.share
  66.6 0.0 copy-start.3
  66.6 9.3 %convolution_convert_fusion = bf16[512,7296]{1,0:T(8,128)(2,1)} fusion(pred[512,512]{1,0:T(32,128)(4,1)S(1)} %bitcast_compare_fusion, bf16[512,7296]{1,0:T(8,128)(2,1)} %all-gather.2.cloned.1.call-done), kind=kOutput, calls=%fused_computation | convolution fusion | flops 3828940800 | bytes 15204352 | tf_op jit(solution)/shard_map/dot_general | solution.py:493
  75.9 0.0 copy-done.3
  75.9 50.0 %shard_map.56 = bf16[2,2,128,768]{3,2,1,0:T(8,128)(2,1)S(1)} custom-call(s32[4]{0:T(128)S(1)} %copy-done.3, bf16[2,2,128,7296]{3,2,1,0:T(8,128)(2,1)} %bitcast.37, f32[2,2,128,1]{3,2,1,0:T(8,128)S(1)} %copy.41.share, bf16[2,7168,1024]{2,1,0:T(8,128)(2,1)} %get-tuple-element.7.gate_w, bf16[2,7168,1024]{2,1,0:T(8,128)(2,1)} %get-tuple-element.8.up_w), custom_call_target="tpu_custom_call" | custom-call | flops 13212057600 | bytes 7471104 | tf_op jit(solution)/shard_map/pallas_call | solution.py:150
  126.0 0.0 copy-start
  126.0 2.9 %collective-permute-start = (bf16[4,128,768]{2,1,0:T(8,128)(2,1)S(1)}, bf16[4,128,768]{2,1,0:T(8,128)(2,1)S(1)}, u32[]{:S(2)}, u32[]{:S(2)}) collective-permute-start(bf16[4,128,768]{2,1,0:T(8,128)(2,1)S(1)} %bitcast.33), channel_id=1, source_target_pairs={{0,8},{8,0},{16,24},{24,16},{1,9},{9,1},{17,25},{25,17},{2,10},{10... | collective-permute-start | bytes 2359304 | tf_op jit(solution)/shard_map/ppermute | solution.py:498
  128.9 0.1 reduce_or.22
  129.0 19.4 %shard_map.57 = bf16[2,2,128,256]{3,2,1,0:T(8,128)(2,1)S(1)} custom-call(s32[4]{0:T(128)S(1)} %copy-done.3, bf16[2,2,128,7296]{3,2,1,0:T(8,128)(2,1)} %bitcast.38, f32[2,2,128,1]{3,2,1,0:T(8,128)S(1)} %copy.41.share, bf16[2,7168,1024]{2,1,0:T(8,128)(2,1)} %get-tuple-element.7.gate_w, bf16[2,7168,1024]{2,1,0:T(8,128)(2,1)} %get-tuple-element.8.up_w), custom_call_target="tpu_custom_call" | custom-call | flops 4404019200 | bytes 7471104 | tf_op jit(solution)/shard_map/pallas_call | solution.py:150
  148.5 0.0 copy-done
  148.5 0.0 copy-start.1
  148.5 0.1 collective-permute-start.1
  148.7 0.1 reshape.59
  148.8 1.9 collective-permute-start.2
  150.7 0.1 stack_reshape.3
  150.8 5.7 %collective-permute-done.2 = s32[512,4]{0,1:T(4,128)S(1)} collective-permute-done((s32[512,4]{0,1:T(4,128)S(1)}, s32[512,4]{0,1:T(4,128)S(1)}, u32[]{:S(2)}, u32[]{:S(2)}) %collective-permute-start.2) | collective-permute-done | bytes 8224 | tf_op jit(solution)/shard_map/ppermute | solution.py:490
  156.5 1.0 copy.45.token_slot
  157.5 0.0 collective-permute-done.1.other_rest
  157.5 0.0 copy-start.5
  157.5 0.0 collective-permute-done.other_main
  157.5 0.0 copy-done.1
  157.5 0.7 copy-done.5
  158.2 0.0 copy-start.4
  158.2 0.9 copy-done.4
  159.1 54.7 %shard_map.58 = bf16[64,7168]{1,0:T(8,128)(2,1)} custom-call(s32[4]{0:T(128)} %seeds.7, bf16[4,128,768]{2,1,0:T(8,128)(2,1)} %bitcast.34, bf16[4,128,256]{2,1,0:T(8,128)(2,1)} %bitcast.36, bf16[4,128,768]{2,1,0:T(8,128)(2,1)} %copy-done.4, bf16[4,128,256]{2,1,0:T(8,128)(2,1)} %copy-done.5, s32[2,512,4]{2,1,0:T(8,128)} %copy.45.token_slot), custom_call_target="tpu_custom_call" | custom-call | flops 17616076800 | bytes 7340032 | tf_op jit(solution)/shard_map/pallas_call | solution.py:402
  213.8 2.2 copy.50
  (16 shorter events, 0.2 us)
Async XLA Ops:
  6.5 57.8 %all-gather.2.cloned.1.call-start = ((), (), s32[]{:S(2)}) async-start(), calls=%async_computation | async-start | bytes 8404992 | tf_op jit(solution)/shard_map/all_gather | solution.py:473
  11.0 0.7 copy-start.2
  66.6 9.4 %copy-start.3 = (s32[4]{0:T(128)S(1)}, s32[4]{0:T(128)}, u32[]{:S(2)}) copy-start(s32[4]{0:T(128)} %seeds.7) | copy-start | bytes 52
  126.0 22.5 %copy-start = (bf16[2,2,128,768]{3,2,1,0:T(8,128)(2,1)}, bf16[2,2,128,768]{3,2,1,0:T(8,128)(2,1)S(1)}, u32[]{:S(2)}) copy-start(bf16[2,2,128,768]{3,2,1,0:T(8,128)(2,1)S(1)} %shard_map.56) | copy-start | bytes 2359300
  126.0 31.6 %collective-permute-start = (bf16[4,128,768]{2,1,0:T(8,128)(2,1)S(1)}, bf16[4,128,768]{2,1,0:T(8,128)(2,1)S(1)}, u32[]{:S(2)}, u32[]{:S(2)}) collective-permute-start(bf16[4,128,768]{2,1,0:T(8,128)(2,1)S(1)} %bitcast.33), channel_id=1, source_target_pairs={{0,8},{8,0},{16,24},{24,16},{1,9},{9,1},{17,25},{25,17},{2,10},{10... | collective-permute-start | bytes 2359304 | tf_op jit(solution)/shard_map/ppermute | solution.py:498
  148.5 9.1 %copy-start.1 = (bf16[2,2,128,256]{3,2,1,0:T(8,128)(2,1)}, bf16[2,2,128,256]{3,2,1,0:T(8,128)(2,1)S(1)}, u32[]{:S(2)}) copy-start(bf16[2,2,128,256]{3,2,1,0:T(8,128)(2,1)S(1)} %shard_map.57) | copy-start | bytes 786436
  148.5 9.0 %collective-permute-start.1 = (bf16[4,128,256]{2,1,0:T(8,128)(2,1)S(1)}, bf16[4,128,256]{2,1,0:T(8,128)(2,1)S(1)}, u32[]{:S(2)}, u32[]{:S(2)}) collective-permute-start(bf16[4,128,256]{2,1,0:T(8,128)(2,1)S(1)} %bitcast.35), channel_id=1, source_target_pairs={{0,8},{8,0},{16,24},{24,16},{1,9},{9,1},{17,25},{25,17},{2,10},{10... | collective-permute-start | bytes 786440 | tf_op jit(solution)/shard_map/ppermute | solution.py:500
  148.8 7.7 %collective-permute-start.2 = (s32[512,4]{0,1:T(4,128)S(1)}, s32[512,4]{0,1:T(4,128)S(1)}, u32[]{:S(2)}, u32[]{:S(2)}) collective-permute-start(s32[512,4]{0,1:T(4,128)S(1)} %reshape.59), channel_id=1, source_target_pairs={{0,8},{8,0},{16,24},{24,16},{1,9},{9,1},{17,25},{25,17},{2,10},{10... | collective-permute-start | bytes 24584 | tf_op jit(solution)/shard_map/ppermute | solution.py:490
  157.5 0.7 copy-start.5
  158.2 0.9 copy-start.4
Sparse Core Ops, SparseCore 0:
  11.0 53.1 all-gather.1
